TPU v7x, 512 devices: a whole 4x8x8 slice. The times are simulated.
512 devices in a mesh: slab: 8 (over y_lo, x), dp: 64 (over y_hi, z, core).
Axes of the slice: x: 4, y: 8 (y_hi: 4, y_lo: 2; y = y_hi * 2 + y_lo), z: 8, core: 2. Of those that a mesh axis runs over, the one named last changes fastest.
Arguments:
- activations: bfloat16 [64, 32, 16, 4096], P('dp', 'slab'), may hold values from -6 to 6
- cotangent: bfloat16 [64, 32, 16, 4096], P('dp', 'slab'), may hold values from -6 to 6
- params: float32 [110592], P(('slab', 'dp')), may hold values from -0.15625 to 0.15625
- moment_one: float32 [110592], P(('slab', 'dp')), may hold values from -0.6 to 0.6
- moment_two: float32 [110592], P(('slab', 'dp')), may hold values from 0.004 to 0.04
Outputs:
- result: bfloat16 [64, 32, 16, 4096], P('dp', 'slab')
- input_grad: bfloat16 [64, 32, 16, 4096], P('dp', 'slab')
- new_params: float32 [110592], P(('slab', 'dp'))
- new_moment_one: float32 [110592], P(('slab', 'dp'))
- new_moment_two: float32 [110592], P(('slab', 'dp'))
All inputs are finite; a program needn't handle non-finite values.
Results may differ from a plain program's by a relative error of at most 0.008.
Values may be sent and summed in bfloat16 or wider, within the bound.
A program may use at most 64 MiB of HBM per device.

v0:
```python
import jax
import jax.numpy as jnp
from jax import lax
from jax.sharding import PartitionSpec as P

C = 64


def with_halo(cells, sides, width):
    for axis, dim in sides:
        count = lax.axis_size(axis)
        ends = count - 1
        head = lax.slice_in_dim(cells, 0, width, axis=dim)
        tail = lax.slice_in_dim(cells, cells.shape[dim] - width, cells.shape[dim], axis=dim)
        cells = jnp.concatenate(
            [
                lax.ppermute(tail, axis, [(i, (i + 1) % count) for i in range(ends)]),
                cells,
                lax.ppermute(head, axis, [((i + 1) % count, i) for i in range(ends)]),
            ],
            axis=dim,
        )
    return cells


def on_device(activations, cotangent, params, moment_one, moment_two):
    samples, planes, rows, packed = activations.shape
    channels = C
    width = packed // channels
    shard = params.astype(jnp.bfloat16)
    gathered = lax.all_gather(shard, ("slab", "dp"), axis=0, tiled=True)
    kernel = gathered.reshape(3, 3, 3, channels, channels)
    numbers = ("NDHWC", "DHWIO", "NDHWC")
    spatial = ((0, 0), (1, 1), (1, 1))
    padded = with_halo(activations, (("slab", 1),), 1)
    seed_pad = with_halo(cotangent, (("slab", 1),), 1)
    padded_five = padded.reshape(samples, planes + 2, rows, width, channels)
    output = lax.conv_general_dilated(
        padded_five,
        kernel,
        (1, 1, 1),
        spatial,
        dimension_numbers=numbers,
        preferred_element_type=jnp.float32,
    )
    result = output.astype(jnp.bfloat16).reshape(samples, planes, rows, packed)
    seed_five = seed_pad.reshape(samples, planes + 2, rows, width, channels)
    flipped = jnp.transpose(kernel[::-1, ::-1, ::-1], (0, 1, 2, 4, 3))
    backward = lax.conv_general_dilated(
        seed_five,
        flipped,
        (1, 1, 1),
        spatial,
        dimension_numbers=numbers,
        preferred_element_type=jnp.float32,
    )
    input_grad = backward.astype(jnp.bfloat16).reshape(samples, planes, rows, packed)
    seed_inner = cotangent.reshape(samples, planes, rows, width, channels)
    kernel_term = lax.conv_general_dilated(
        padded_five,
        seed_inner,
        (1, 1, 1),
        spatial,
        dimension_numbers=("CDHWN", "IDHWO", "NDHWC"),
        preferred_element_type=jnp.float32,
    )
    flat_term = jnp.transpose(kernel_term, (1, 2, 3, 0, 4)).reshape(-1)
    summed = lax.psum_scatter(flat_term, ("slab", "dp"), scatter_dimension=0, tiled=True)
    cells = samples * lax.axis_size("dp") * planes * lax.axis_size("slab") * rows * width
    grad = summed / jnp.sqrt(jnp.float32(cells))
    new_one = 0.9 * moment_one + 0.1 * grad
    new_two = 0.999 * moment_two + 0.001 * grad * grad
    update = 3.0 * (new_one / (1.0 - 0.9**10)) / (jnp.sqrt(new_two / (1.0 - 0.999**10)) + 1e-08)
    return (result, input_grad, params - update, new_one, new_two)


def solution(mesh):
    placed = (
        P("dp", "slab", None, None),
        P("dp", "slab", None, None),
        P(("slab", "dp")),
        P(("slab", "dp")),
        P(("slab", "dp")),
    )
    return jax.shard_map(
        on_device,
        mesh=mesh,
        in_specs=placed,
        out_specs=(
            P("dp", "slab", None, None),
            P("dp", "slab", None, None),
            P(("slab", "dp")),
            P(("slab", "dp")),
            P(("slab", "dp")),
        ),
        check_vma=False,
    )
```

profile of v0, /device:TPU:1, one launch (start us, length us, event | category | flops | bytes accessed | tf_op | source)
XLA Modules:
  0.0 626.9 jit_solution(14151081716052048402)
XLA Ops:
  7.2 0.0 all-reduce.7.cloned.1.call-start
  7.2 1.7 fusion.29
  8.9 4.6 collective-permute-start
  13.5 1.3 collective-permute-start.1
  14.8 4.4 reshape.69
  19.2 0.0 collective-permute-done
  19.2 0.9 constant_dynamic-update-slice_fusion.2
  20.1 0.0 collective-permute-done.1
  20.2 0.0 copy-start
  20.2 5.6 reshape.68
  25.8 28.5 %fusion.30 = f32[3,3,3,64,64]{4,3,2,1,0:T(8,128)} fusion(bf16[1,6,16,64,64]{4,0,3,2,1:T(2,128)(2,1)} %reshape.68, bf16[1,4,16,64,64]{4,0,3,2,1:T(2,128)(2,1)S(1)} %reshape.69), kind=kOutput, calls=%fused_computation.34 | convolution fusion | flops 859176960 | bytes 1753088 | tf_op jit(solution)/shard_map/transpose | solution.py:67
  54.2 2.1 reshape.37
  56.4 0.0 all-reduce.7.cloned.1.call-update
  56.4 0.0 all-reduce.5.cloned.1.call-start
  56.5 4.1 collective-permute-start.2
  60.6 1.3 collective-permute-start.3
  61.9 268.9 %all-reduce.7.cloned.1.call-done = f32[110592]{0:T(1024)} async-done(((f32[110592]{0:T(1024)}), f32[110592]{0:T(1024)}) %all-reduce.7.cloned.1.call-update) | async-done | bytes 442384
  330.8 1.4 divide_subtract_fusion
  332.2 0.2 dynamic-update-slice
  332.4 0.7 copy-done.4
  333.1 0.0 all-reduce.5.cloned.1.call-update
  333.2 0.0 collective-permute-done.2
  333.2 0.0 collective-permute-done.3
  333.2 0.1 pad_maximum_fusion
  333.3 1.7 reshape.52
  335.0 1.0 copy.43
  336.1 0.3 pad.clone
  336.4 1.7 copy.33
  338.1 1.9 slice.20
  339.9 1.9 reshape.58
  341.9 1.0 copy.44
  342.9 0.3 pad.2.clone
  343.2 0.0 copy-start.5
  343.3 0.0 copy-start.9
  343.3 0.5 copy.38
  343.7 0.9 slice.22
  344.6 253.6 %all-reduce.5.cloned.1.call-done = bf16[110592]{0:T(1024)(128)(2,1)} async-done(((bf16[110592]{0:T(1024)(128)(2,1)}), bf16[110592]{0:T(1024)(128)(2,1)}) %all-reduce.5.cloned.1.call-update) | async-done | bytes 221200
  598.2 1.1 reshape.32
  599.4 6.0 select_convert_fusion.1
  605.4 0.2 copy.34
  605.6 0.2 slice.21
  605.8 0.3 copy.35
  606.1 1.6 reshape.33
  607.7 9.7 %select_convert_fusion = bf16[4,16,8,9,64]{4,2,3,1,0:T(8,128)(2,1)S(1)} fusion(bf16[3,3,3,64,64]{4,3,2,1,0:T(8,128)(2,1)S(1)} %reshape.32, bf16[6,16,1,7,2,64]{5,3,4,1,0,2:T(8,128)(2,1)} %slice.22, bf16[6,16,1,8,9,64]{5,3,4,1,0,2:T(8,128)(2,1)S(1)} %copy.38, pred[8,9]{0,1:T(8,128)(4,1)S(1)} %copy-done.9), kind=kOutput, calls=%fused_computation.3 | convolution fusion | flops 980582400 | bytes 1867848 | tf_op jit(solution)/shard_map/conv_general_dilated | solution.py:49
  617.3 0.2 copy.39
  617.5 0.2 slice.23
  617.7 0.3 copy.40
  618.0 1.6 reshape.35
  (20 shorter events, 0.1 us)
Async XLA Ops:
  7.2 12.9 %copy-start.3 = (bf16[1,4,16,4096]{3,2,1,0:T(8,128)(2,1)S(1)}, bf16[1,4,16,4096]{3,2,1,0:T(8,128)(2,1)}, u32[]{:S(2)}) copy-start(bf16[1,4,16,4096]{3,2,1,0:T(8,128)(2,1)} %param.5) | copy-start | bytes 1572868
  7.2 323.6 %all-reduce.7.cloned.1.call-start = ((), (), s32[]{:S(2)}) async-start(), calls=%async_computation.1 | async-start | bytes 884736
  8.9 10.3 %collective-permute-start = (bf16[1,1,16,4096]{3,2,1,0:T(8,128)(2,1)S(1)}, bf16[1,1,16,4096]{3,2,1,0:T(8,128)(2,1)}, u32[]{:S(2)}, u32[]{:S(2)}) collective-permute-start(bf16[1,1,16,4096]{3,2,1,0:T(8,128)(2,1)S(1)} %get-tuple-element.11), channel_id=1, source_target_pairs={{0,64},{64,128},{128,192},{192,256},{256,320},{320,384},{384,448},... | collective-permute-start | bytes 393224 | tf_op jit(solution)/shard_map/ppermute | solution.py:17
  13.5 6.6 %collective-permute-start.1 = (bf16[1,1,16,4096]{3,2,1,0:T(8,128)(2,1)}, bf16[1,1,16,4096]{3,2,1,0:T(8,128)(2,1)S(1)}, u32[]{:S(2)}, u32[]{:S(2)}) collective-permute-start(bf16[1,1,16,4096]{3,2,1,0:T(8,128)(2,1)} %get-tuple-element.10), channel_id=1, source_target_pairs={{64,0},{128,64},{192,128},{256,192},{320,256},{384,320},{448,384},... | collective-permute-start | bytes 393224 | tf_op jit(solution)/shard_map/ppermute | solution.py:19
  20.2 34.1 %copy-start = (bf16[1,6,16,4096]{3,2,1,0:T(8,128)(2,1)}, bf16[1,6,16,4096]{3,2,1,0:T(8,128)(2,1)S(1)}, u32[]{:S(2)}) copy-start(bf16[1,6,16,4096]{3,2,1,0:T(8,128)(2,1)S(1)} %constant_dynamic-update-slice_fusion) | copy-start | bytes 2359300
  25.8 30.7 %copy-start.2 = (bf16[1,4,16,4096]{3,2,1,0:T(8,128)(2,1)S(1)}, bf16[1,4,16,4096]{3,2,1,0:T(8,128)(2,1)}, u32[]{:S(2)}) copy-start(bf16[1,4,16,4096]{3,2,1,0:T(8,128)(2,1)} %param.6) | copy-start | bytes 1572868
  54.2 276.6 %copy-start.6 = (f32[216]{0:T(256)S(1)}, f32[216]{0:T(256)}, u32[]{:S(2)}) copy-start(f32[216]{0:T(256)} %param.7) | copy-start | bytes 2596
  54.2 276.6 %copy-start.7 = (f32[216]{0:T(256)S(1)}, f32[216]{0:T(256)}, u32[]{:S(2)}) copy-start(f32[216]{0:T(256)} %param.8) | copy-start | bytes 2596
  54.2 276.6 %copy-start.8 = (f32[216]{0:T(256)S(1)}, f32[216]{0:T(256)}, u32[]{:S(2)}) copy-start(f32[216]{0:T(256)} %param.9) | copy-start | bytes 2596
  56.4 276.9 %copy-start.1 = (bf16[1,6,16,4096]{3,2,1,0:T(8,128)(2,1)S(1)}, bf16[1,6,16,4096]{3,2,1,0:T(8,128)(2,1)}, u32[]{:S(2)}) copy-start(bf16[1,6,16,4096]{3,2,1,0:T(8,128)(2,1)} %copy-done) | copy-start | bytes 2359300
  56.4 541.8 %all-reduce.5.cloned.1.call-start = ((), (), s32[]{:S(2)}) async-start(), calls=%async_computation | async-start | bytes 442368
  56.5 276.6 %collective-permute-start.2 = (bf16[1,1,16,4096]{3,2,1,0:T(8,128)(2,1)S(1)}, bf16[1,1,16,4096]{3,2,1,0:T(8,128)(2,1)S(1)}, u32[]{:S(2)}, u32[]{:S(2)}) collective-permute-start(bf16[1,1,16,4096]{3,2,1,0:T(8,128)(2,1)S(1)} %get-tuple-element.8), channel_id=1, source_target_pairs={{0,64},{64,128},{128,192},{192,256},{256,320},{320,384},{384,448},... | collective-permute-start | bytes 393224 | tf_op jit(solution)/shard_map/ppermute | solution.py:17
  60.6 272.5 %collective-permute-start.3 = (bf16[1,1,16,4096]{3,2,1,0:T(8,128)(2,1)S(1)}, bf16[1,1,16,4096]{3,2,1,0:T(8,128)(2,1)S(1)}, u32[]{:S(2)}, u32[]{:S(2)}) collective-permute-start(bf16[1,1,16,4096]{3,2,1,0:T(8,128)(2,1)S(1)} %get-tuple-element.9), channel_id=1, source_target_pairs={{64,0},{128,64},{192,128},{256,192},{320,256},{384,320},{448,384},... | collective-permute-start | bytes 393224 | tf_op jit(solution)/shard_map/ppermute | solution.py:19
  332.4 0.7 copy-start.4
  343.2 256.2 %copy-start.5 = (bf16[6,16,1,7,2,64]{5,3,4,1,0,2:T(8,128)(2,1)S(1)}, bf16[6,16,1,7,2,64]{5,3,4,1,0,2:T(8,128)(2,1)}, u32[]{:S(2)}) copy-start(bf16[6,16,1,7,2,64]{5,3,4,1,0,2:T(8,128)(2,1)} %slice.20) | copy-start | bytes 516100
  343.3 256.2 %copy-start.9 = (pred[8,9]{0,1:T(8,128)(4,1)S(1)}, pred[8,9]{0,1:T(8,128)(4,1)}, u32[]{:S(2)}) copy-start(pred[8,9]{0,1:T(8,128)(4,1)} %constant.36) | copy-start | bytes 220
Sparse Core Ops, SparseCore 0:
  56.5 274.2 all-reduce.6
  337.1 261.0 all-reduce.4
where the time goes:
time: 636 us; the launch traced here: 627 us
  waiting for transfers between devices  523 us (82%)
  matrix products  44.1 us (7%)
  local copies, waits for them, and re-layouts  32.6 us (5%)
  between operations  14.8 us (2%)
  starting transfers between devices  11.4 us (2%)
    unnamed x4, waiting for transfers between devices  523 us
    transpose x1, matrix products, on_device(): flat_term = jnp.transpose(kernel_term, (1, 2, 3, 0, 4)).reshape(-1)  28.5 us
  transfers between devices with their start and end apart: 6, of which 2 were waited for; matrix products, arithmetic and copies ran while one was open for 3% of the time, Pallas kernels for 0%

commit v1 on v0

v1 whole, which is shorter than its diff:
```python
import jax
import jax.numpy as jnp
from jax import lax
from jax.experimental import pallas as pl
from jax.experimental.pallas import tpu as pltpu
from jax.sharding import PartitionSpec as P

MESH = pl.DeviceIdType.MESH
F32 = jnp.float32
BF16 = jnp.bfloat16
SHARE = 216
PLANE = 512


def place():
    slab, dp = lax.axis_index("slab"), lax.axis_index("dp")
    return {
        "slab": slab,
        "dp": dp,
        "t": slab // 2,
        "u": (slab % 2) * 4 + dp // 16,
        "z": (dp // 2) % 8,
        "core": dp % 2,
    }


def u_peer(me, d):
    other = (me["u"] + d) % 8
    return ((me["slab"] // 2) * 2 + other // 4, (other % 4) * 16 + me["dp"] % 16)


def t_peer(me, d):
    return (((me["t"] + d) % 4) * 2 + me["slab"] % 2, me["dp"])


def z_peer(me, d):
    return (me["slab"], (me["dp"] // 16) * 16 + ((me["z"] + d) % 8) * 2 + me["core"])


def core_peer(me):
    return (me["slab"], me["dp"] + 1 - 2 * me["core"])


def slab_peer(me, d):
    return ((me["slab"] + d) % 8, me["dp"])


def greet(peers):
    barrier = pltpu.get_barrier_semaphore()
    for peer in peers:
        pl.semaphore_signal(barrier, inc=1, device_id=peer, device_id_type=MESH)
    pl.semaphore_wait(barrier, len(peers))


def share_peers(me):
    return (
        [u_peer(me, d) for d in range(1, 8)]
        + [t_peer(me, d) for d in range(1, 4)]
        + [z_peer(me, d) for d in range(1, 8)]
        + [core_peer(me)]
    )


def remote(src, dst, sems, index, peer):
    return pltpu.make_async_remote_copy(
        src_ref=src,
        dst_ref=dst,
        send_sem=sems.at[0, index],
        recv_sem=sems.at[1, index],
        device_id=peer,
        device_id_type=MESH,
    )


def start(copies):
    for copy in copies:
        copy.start()
    return copies


def wait_recv(copies):
    for copy in copies:
        copy.wait_recv()


def wait_send(copies):
    for copy in copies:
        copy.wait_send()


def iota(shape, axis):
    return lax.broadcasted_iota(jnp.int32, shape, axis)


def gather_kernel(act, cot, par, act_pad, cot_pad, weights, act_buf, cot_buf, row, rows, tiles, wide, local, hs, us, ts, zs, cs):
    me = place()
    greet(share_peers(me) + [slab_peer(me, 1), slab_peer(me, 7)])
    row[...] = jnp.zeros_like(row)
    row[0:1, 0:SHARE] = par[...]
    own = jnp.broadcast_to(row[0:1, :], (8, 256))
    row[...] = jnp.where(iota((8, 256), 0) == me["u"], own, 0.0)
    first = start([remote(row, rows.at[d - 1], us, d - 1, u_peer(me, d)) for d in range(1, 8)])
    halo = []
    for k, (src, buf) in enumerate(((act, act_buf), (cot, cot_buf))):
        halo.append(remote(src.at[3], buf.at[0], hs, 2 * k, slab_peer(me, 1)))
        halo.append(remote(src.at[0], buf.at[5], hs, 2 * k + 1, slab_peer(me, 7)))
    start(halo)
    inner = []
    for k, (src, pad) in enumerate(((act, act_pad), (cot, cot_pad))):
        inner.append(pltpu.make_async_copy(src, pad.at[pl.ds(1, 4)], local.at[k]))
    start(inner)
    wait_recv(first)
    tile = row[...]
    for d in range(7):
        tile = tile + rows[d]
    tiles[me["t"]] = tile
    second = start([remote(tiles.at[me["t"]], tiles.at[me["t"]], ts, d - 1, t_peer(me, d)) for d in range(1, 4)])
    wait_recv(second)
    wide[me["core"], me["z"]] = jnp.concatenate([tiles[k] for k in range(4)], axis=0).astype(BF16)
    mine = wide.at[me["core"], me["z"]]
    third = start([remote(mine, mine, zs, d - 1, z_peer(me, d)) for d in range(1, 8)])
    wait_recv(third)
    half = wide.at[me["core"]]
    fourth = start([remote(half, half, cs, 0, core_peer(me))])
    wait_recv(halo)
    for buf, pad in ((act_buf, act_pad), (cot_buf, cot_pad)):
        low, high = buf[0], buf[5]
        pad[0] = jnp.where(me["slab"] == 0, jnp.zeros_like(low), low)
        pad[5] = jnp.where(me["slab"] == 7, jnp.zeros_like(high), high)
    wait_recv(fourth)
    weights[...] = wide[...]
    for copy in inner:
        copy.wait()
    wait_send(first + halo + second + third + fourth)


def gather(act, cot, par):
    vmem = pl.BlockSpec(memory_space=pltpu.VMEM)
    planes = jax.ShapeDtypeStruct((6, 16, 4096), BF16)
    return pl.pallas_call(
        gather_kernel,
        out_shape=(planes, planes, jax.ShapeDtypeStruct((2, 8, 32, 256), BF16)),
        in_specs=[vmem] * 3,
        out_specs=(vmem,) * 3,
        scratch_shapes=[
            pltpu.VMEM((6, 16, 4096), BF16),
            pltpu.VMEM((6, 16, 4096), BF16),
            pltpu.VMEM((8, 256), F32),
            pltpu.VMEM((7, 8, 256), F32),
            pltpu.VMEM((4, 8, 256), F32),
            pltpu.VMEM((2, 8, 32, 256), BF16),
            pltpu.SemaphoreType.DMA((2,)),
            pltpu.SemaphoreType.DMA((2, 4)),
            pltpu.SemaphoreType.DMA((2, 7)),
            pltpu.SemaphoreType.DMA((2, 3)),
            pltpu.SemaphoreType.DMA((2, 7)),
            pltpu.SemaphoreType.DMA((2, 1)),
        ],
        compiler_params=pltpu.CompilerParams(
            collective_id=0, has_side_effects=True, vmem_limit_bytes=32 * 2**20
        ),
    )(act, cot, par)


def spread(field, out, p):
    moved = pltpu.roll(field[p].astype(F32), 64, 1)
    lane = iota((16, 128), 1)
    line = iota((16, 128), 0)
    base = p * PLANE if isinstance(p, int) else pl.multiple_of(p * PLANE, PLANE)
    for chunk in range(33):
        if chunk == 0:
            cells = jnp.where(lane >= 64, moved[:, 0:128], 0.0)
        elif chunk == 32:
            cells = jnp.where(lane < 64, moved[:, 0:128], 0.0)
        else:
            cells = moved[:, 128 * chunk : 128 * chunk + 128]
        above = jnp.where(line > 0, pltpu.roll(cells, 1, 0), 0.0)
        below = jnp.where(line < 15, pltpu.roll(cells, 15, 0), 0.0)
        for ky, part in enumerate((above, cells, below)):
            part = part.astype(BF16)
            if chunk < 32:
                out[pl.ds(base + 16 * chunk, 16), 256 * ky : 256 * ky + 128] = part
            if chunk > 0:
                out[pl.ds(base + 16 * (chunk - 1), 16), 256 * ky + 128 : 256 * ky + 256] = part


def turn(field, out, p):
    plane = field[p]
    stacked = jnp.concatenate([plane[:, 128 * g : 128 * g + 128] for g in range(32)], axis=0)
    out[pl.ds((p - 1) * 128, 128), :] = stacked.T


def kernel_gradient(turned, spread_cot, total):
    for p in (2, 3, 1, 4, 0, 5):
        low, high = max(0, 2 - p), min(2, 5 - p)
        first, count = p - 2 + low, high - low + 1
        term = jnp.dot(
            turned[first * 128 : (first + count) * 128, :],
            spread_cot[p * PLANE : (p + 1) * PLANE, :],
            preferred_element_type=F32,
        )
        if p == 2:
            total[...] = term
        else:
            total[low * 128 : (high + 1) * 128, :] += term


def fold(total, flat):
    for kz in range(3):
        for ky in range(3):
            at = 256 * (2 - ky)
            left = total[kz * 128 : kz * 128 + 64, at : at + 256]
            right = total[kz * 128 + 64 : kz * 128 + 128, at : at + 256]
            both = left + pltpu.roll(right, 192, 1)
            row = (kz * 3 + ky) * 3 * 64
            flat[row : row + 64, :] = both[:, 128:256]
            flat[row + 64 : row + 128, :] = pltpu.roll(both[:, 0:128], 64, 1)
            flat[row + 128 : row + 192, :] = both[:, 0:128]


def to_shares(flat, shares):
    lane = iota((32, 128), 1)
    for zh in range(2):
        source = [flat[pl.ds(27 * zh + r, 32, stride=54), :] for r in range(27)]
        for s in range(8):
            halves = [jnp.zeros((32, 128), F32), jnp.zeros((32, 128), F32)]
            for r in range(SHARE * s // 64, (SHARE * s + SHARE - 1) // 64 + 1):
                at = 64 * r - SHARE * s
                moved = pltpu.roll(source[r], at % 128, 1) if at % 128 else source[r]
                low, high = max(at, 0), min(at + 64, SHARE)
                for h in range(2):
                    begin, end = max(low - 128 * h, 0), min(high - 128 * h, 128)
                    if begin < end:
                        halves[h] = jnp.where((lane >= begin) & (lane < end), moved, halves[h])
            for h in range(2):
                shares[s % 2, zh * 4 + s // 2, :, 128 * h : 128 * h + 128] = halves[h]


def from_shares(shares, flat):
    lane = iota((32, 128), 1)
    for zh in range(2):
        source = [
            [shares[s % 2, zh * 4 + s // 2, :, 128 * h : 128 * h + 128].astype(F32) for h in range(2)]
            for s in range(8)
        ]
        for r in range(27):
            out = jnp.zeros((32, 128), F32)
            for s in range(64 * r // SHARE, (64 * r + 63) // SHARE + 1):
                shift = SHARE * s - 64 * r
                low, high = max(64 * r, SHARE * s) - SHARE * s, min(64 * r + 64, SHARE * (s + 1)) - SHARE * s
                for h in range(2):
                    begin, end = max(low, 128 * h), min(high, 128 * h + 128)
                    if begin < end:
                        by = (shift + 128 * h) % 128
                        moved = pltpu.roll(source[s][h], by, 1) if by else source[s][h]
                        out = jnp.where((lane >= begin + shift) & (lane < end + shift), moved, out)
            flat[pl.ds(27 * zh + r, 32, stride=54), :] = out


def bands(flat, forward, backward):
    for kz in range(3):
        for ky in range(3):
            row = (kz * 3 + ky) * 3 * 64
            taps = [flat[row + 64 * kx : row + 64 * kx + 64, :] for kx in range(3)]
            moved = [pltpu.roll(tap, 64, 1) for tap in taps]
            at = kz * 768 + ky * 256
            blocks = (taps[0], taps[1] + moved[0], taps[2] + moved[1], moved[2])
            forward[at : at + 256, :] = jnp.concatenate(blocks, axis=0).astype(BF16)
            at = (2 - kz) * 768 + (2 - ky) * 256
            left = jnp.concatenate([taps[2] + moved[1], moved[2]], axis=0)
            right = jnp.concatenate([taps[0], taps[1] + moved[0]], axis=0)
            backward[at : at + 128, :] = left.T.astype(BF16)
            backward[at + 128 : at + 256, :] = right.T.astype(BF16)


def convolve(spread_field, band, out, z):
    total = None
    for kz in range(3):
        at = (z + kz) * PLANE if isinstance(z, int) else pl.multiple_of((z + kz) * PLANE, PLANE)
        term = jnp.dot(
            spread_field[pl.ds(at, PLANE), :],
            band[kz * 768 : kz * 768 + 768, :],
            preferred_element_type=F32,
        )
        total = term if total is None else total + term
    rounded = total.astype(BF16)
    for g in range(32):
        out[z, :, 128 * g : 128 * g + 128] = rounded[16 * g : 16 * g + 16, :]


def compute_kernel(act, cot, weights, result, input_grad, shares, a3, b3, turned, total, flat, forward, backward):
    @pl.loop(0, 6)
    def _(p):
        spread(act, a3, p)
        spread(cot, b3, p)

    for p in range(1, 5):
        turn(act, turned, p)
    kernel_gradient(turned, b3, total)
    fold(total, flat)
    to_shares(flat, shares)
    from_shares(weights, flat)
    bands(flat, forward, backward)

    @pl.loop(0, 4)
    def _(z):
        convolve(a3, forward, result, z)
        convolve(b3, backward, input_grad, z)


def compute(act, cot, weights):
    vmem = pl.BlockSpec(memory_space=pltpu.VMEM)
    planes = jax.ShapeDtypeStruct((4, 16, 4096), BF16)
    return pl.pallas_call(
        compute_kernel,
        out_shape=(planes, planes, jax.ShapeDtypeStruct((2, 8, 32, 256), F32)),
        in_specs=[vmem] * 3,
        out_specs=(vmem,) * 3,
        scratch_shapes=[
            pltpu.VMEM((6 * PLANE, 768), BF16),
            pltpu.VMEM((6 * PLANE, 768), BF16),
            pltpu.VMEM((512, 512), BF16),
            pltpu.VMEM((384, 768), F32),
            pltpu.VMEM((1728, 128), F32),
            pltpu.VMEM((2304, 128), BF16),
            pltpu.VMEM((2304, 128), BF16),
        ],
        compiler_params=pltpu.CompilerParams(vmem_limit_bytes=48 * 2**20),
    )(act, cot, weights)


def update_kernel(shares, par, one, two, new_par, new_one, new_two, got, mine, sent, parts, tile, tiles, row, rows, us, ts, zs, cs):
    me = place()
    greet(share_peers(me))
    first = start([remote(shares.at[1 - me["core"]], got, cs, 0, core_peer(me))])
    wait_recv(first)
    for k in range(8):
        both = shares[me["core"], k] + got[k]
        mine[k] = both
        sent[k] = both.astype(BF16)
    second = start(
        [remote(sent.at[(me["z"] + d) % 8], parts.at[d - 1], zs, d - 1, z_peer(me, d)) for d in range(1, 8)]
    )
    wait_recv(second)
    total = mine[me["z"]]
    for d in range(7):
        total = total + parts[d].astype(F32)
    for k in range(4):
        tile[k] = total[8 * k : 8 * k + 8, :]
    third = start([remote(tile.at[(me["t"] + d) % 4], tiles.at[d - 1], ts, d - 1, t_peer(me, d)) for d in range(1, 4)])
    wait_recv(third)
    row[...] = tile[me["t"]] + tiles[0] + tiles[1] + tiles[2]
    fourth = start([remote(row, rows.at[d - 1], us, d - 1, u_peer(me, d)) for d in range(1, 8)])
    wait_recv(fourth)
    total = row[...]
    for d in range(7):
        total = total + rows[d]
    share = jnp.sum(jnp.where(iota((8, 256), 0) == me["u"], total, 0.0), axis=0, keepdims=True)
    grad = share[:, 0:SHARE] / jnp.sqrt(F32(64 * 32 * 16 * 64))
    first_moment = 0.9 * one[...] + 0.1 * grad
    second_moment = 0.999 * two[...] + 0.001 * grad * grad
    step = 3.0 * (first_moment / (1.0 - 0.9**10)) / (jnp.sqrt(second_moment / (1.0 - 0.999**10)) + 1e-08)
    new_par[...] = par[...] - step
    new_one[...] = first_moment
    new_two[...] = second_moment
    wait_send(first + second + third + fourth)


def update(shares, par, one, two):
    vmem = pl.BlockSpec(memory_space=pltpu.VMEM)
    share = jax.ShapeDtypeStruct((1, SHARE), F32)
    return pl.pallas_call(
        update_kernel,
        out_shape=(share,) * 3,
        in_specs=[vmem] * 4,
        out_specs=(vmem,) * 3,
        scratch_shapes=[
            pltpu.VMEM((8, 32, 256), F32),
            pltpu.VMEM((8, 32, 256), F32),
            pltpu.VMEM((8, 32, 256), BF16),
            pltpu.VMEM((7, 32, 256), BF16),
            pltpu.VMEM((4, 8, 256), F32),
            pltpu.VMEM((3, 8, 256), F32),
            pltpu.VMEM((8, 256), F32),
            pltpu.VMEM((7, 8, 256), F32),
            pltpu.SemaphoreType.DMA((2, 7)),
            pltpu.SemaphoreType.DMA((2, 3)),
            pltpu.SemaphoreType.DMA((2, 7)),
            pltpu.SemaphoreType.DMA((2, 1)),
        ],
        compiler_params=pltpu.CompilerParams(
            collective_id=1, has_side_effects=True, vmem_limit_bytes=32 * 2**20
        ),
    )(shares, par, one, two)


def on_device(activations, cotangent, params, moment_one, moment_two):
    act, cot = activations[0], cotangent[0]
    par, one, two = (a.reshape(1, SHARE) for a in (params, moment_one, moment_two))
    act_pad, cot_pad, weights = gather(act, cot, par)
    result, input_grad, shares = compute(act_pad, cot_pad, weights)
    new_par, new_one, new_two = update(shares, par, one, two)
    return (
        result[None],
        input_grad[None],
        new_par.reshape(SHARE),
        new_one.reshape(SHARE),
        new_two.reshape(SHARE),
    )


def solution(mesh):
    field, share = P("dp", "slab", None, None), P(("slab", "dp"))
    return jax.shard_map(
        on_device,
        mesh=mesh,
        in_specs=(field, field, share, share, share),
        out_specs=(field, field, share, share, share),
        check_vma=False,
    )
```

time: 636 us -> 68.5 us (0.11)
  the two profiles are of different devices: /device:TPU:1 before, /device:TPU:4 now
where the time goes in v1:
time: 68.5 us; the launch traced here: 68.2 us
  Pallas kernels  62.4 us (91%)
  local copies, waits for them, and re-layouts  5.13 us (7%)
    pallas_call x1, Pallas kernels, gather(): pl.pallas_call(gather_kernel, out_shape=(planes, planes, jax.ShapeDtypeSt...  29.1 us
    pallas_call x1, Pallas kernels, update(): pl.pallas_call(update_kernel, out_shape=(share,) * 3, in_specs=[vmem] * 4...  22.8 us
    pallas_call x1, Pallas kernels, compute(): pl.pallas_call(compute_kernel, out_shape=(planes, planes, jax.ShapeDtypeS...  10.4 us
    unnamed x13, local copies, waits for them, and re-layouts  5.13 us

profile of v1, /device:TPU:4, one launch (start us, length us, event | category | flops | bytes accessed | tf_op | source)
XLA Modules:
  0.0 68.2 jit_solution(4069910454875115149)
XLA Ops:
  0.6 0.0 copy-start.2
  0.6 0.7 copy-done.2
  1.3 0.0 copy-start
  1.3 1.0 %copy-done = bf16[1,4,16,4096]{3,2,1,0:T(8,128)(2,1)S(1)} copy-done((bf16[1,4,16,4096]{3,2,1,0:T(8,128)(2,1)S(1)}, bf16[1,4,16,4096]{3,2,1,0:T(8,128)(2,1)}, u32[]{:S(2)}) %copy-start) | copy-done | bytes 524312
  2.4 0.0 copy-start.1
  2.4 1.0 %copy-done.1 = bf16[1,4,16,4096]{3,2,1,0:T(8,128)(2,1)S(1)} copy-done((bf16[1,4,16,4096]{3,2,1,0:T(8,128)(2,1)S(1)}, bf16[1,4,16,4096]{3,2,1,0:T(8,128)(2,1)}, u32[]{:S(2)}) %copy-start.1) | copy-done | bytes 524312
  3.4 29.1 %shard_map.92 = (bf16[6,16,4096]{2,1,0:T(8,128)(2,1)S(1)}, bf16[6,16,4096]{2,1,0:T(8,128)(2,1)S(1)}, bf16[2,8,32,256]{3,2,1,0:T(8,128)(2,1)S(1)}) custom-call(bf16[4,16,4096]{2,1,0:T(8,128)(2,1)S(1)} %bitcast.10, bf16[4,16,4096]{2,1,0:T(8,128)(2,1)S(1)} %bitcast.11, f32[1,216]{1,0:T(1,128)S(1)} %bitcast.12), custom_call_target="tpu_custom_call" | custom-call | tf_op jit(solution)/shard_map/pallas_call | solution.py:140
  32.5 0.0 copy-start.4
  32.6 10.4 %shard_map.93 = (bf16[4,16,4096]{2,1,0:T(8,128)(2,1)}, bf16[4,16,4096]{2,1,0:T(8,128)(2,1)}, f32[2,8,32,256]{3,2,1,0:T(8,128)S(1)}) custom-call(bf16[6,16,4096]{2,1,0:T(8,128)(2,1)S(1)} %get-tuple-element.14.act, bf16[6,16,4096]{2,1,0:T(8,128)(2,1)S(1)} %get-tuple-element.15.cot, bf16[2,8,32,256]{3,2,1,0:T(8,128)(2,1)S(1)} %get-tuple-element.16.weights), custom_call_target="tpu_custom_call" | custom-call | tf_op jit(solution)/shard_map/pallas_call | solution.py:314
  43.0 0.0 copy-start.3
  43.0 0.0 copy-done.4
  43.0 0.7 copy-done.3
  43.7 22.8 %shard_map.94 = (f32[1,216]{1,0:T(1,128)S(1)}, f32[1,216]{1,0:T(1,128)S(1)}, f32[1,216]{1,0:T(1,128)S(1)}) custom-call(f32[2,8,32,256]{3,2,1,0:T(8,128)S(1)} %get-tuple-element.19.shares, f32[1,216]{1,0:T(1,128)S(1)} %bitcast.13, f32[1,216]{1,0:T(1,128)S(1)} %bitcast.14, f32[1,216]{1,0:T(1,128)S(1)} %bitcast.15), custom_call_target="tpu_custom_call" | custom-call | tf_op jit(solution)/shard_map/pallas_call | solution.py:372
  66.5 0.6 copy.13
  67.1 0.6 copy.14
  67.6 0.6 copy.15
Async XLA Ops:
  0.6 0.7 copy-start.2
  1.3 1.0 %copy-start = (bf16[1,4,16,4096]{3,2,1,0:T(8,128)(2,1)S(1)}, bf16[1,4,16,4096]{3,2,1,0:T(8,128)(2,1)}, u32[]{:S(2)}) copy-start(bf16[1,4,16,4096]{3,2,1,0:T(8,128)(2,1)} %param.5) | copy-start | bytes 1572868
  2.4 1.0 %copy-start.1 = (bf16[1,4,16,4096]{3,2,1,0:T(8,128)(2,1)S(1)}, bf16[1,4,16,4096]{3,2,1,0:T(8,128)(2,1)}, u32[]{:S(2)}) copy-start(bf16[1,4,16,4096]{3,2,1,0:T(8,128)(2,1)} %param.6) | copy-start | bytes 1572868
  32.5 10.5 %copy-start.4 = (f32[216]{0:T(256)S(1)}, f32[216]{0:T(256)}, u32[]{:S(2)}) copy-start(f32[216]{0:T(256)} %param.9) | copy-start | bytes 2596
  43.0 0.7 copy-start.3

commit v2 on v1

v2 whole, which is shorter than its diff:
```python
import jax
import jax.numpy as jnp
from jax import lax
from jax.experimental import pallas as pl
from jax.experimental.pallas import tpu as pltpu
from jax.sharding import PartitionSpec as P

MESH = pl.DeviceIdType.MESH
F32 = jnp.float32
BF16 = jnp.bfloat16
SHARE = 216
PLANE = 512


def place():
    slab, dp = lax.axis_index("slab"), lax.axis_index("dp")
    return {
        "slab": slab,
        "dp": dp,
        "x": slab % 4,
        "y": (dp // 16) * 2 + slab // 4,
        "row": slab * 4 + dp // 16,
        "z": (dp // 2) % 8,
        "core": dp % 2,
    }


def hops(d, n):
    return min(d, n - d)


XY = sorted(
    [(dx, dy) for dx in range(4) for dy in range(8) if dx or dy],
    key=lambda o: -(hops(o[0], 4) + hops(o[1], 8)),
)
Z = sorted(range(1, 8), key=lambda d: -hops(d, 8))


def xy_peer(me, offset):
    x, y = (me["x"] + offset[0]) % 4, (me["y"] + offset[1]) % 8
    return ((y % 2) * 4 + x, (y // 2) * 16 + me["dp"] % 16)


def xy_row(me, offset):
    slab, dp = xy_peer(me, offset)
    return slab * 4 + dp // 16


def z_peer(me, d):
    return (me["slab"], (me["dp"] // 16) * 16 + ((me["z"] + d) % 8) * 2 + me["core"])


def core_peer(me):
    return (me["slab"], me["dp"] + 1 - 2 * me["core"])


def slab_peer(me, d):
    return ((me["slab"] + d) % 8, me["dp"])


def remote(src, dst, sems, index, peer):
    return pltpu.make_async_remote_copy(
        src_ref=src,
        dst_ref=dst,
        send_sem=sems.at[0, index],
        recv_sem=sems.at[1, index],
        device_id=peer,
        device_id_type=MESH,
    )


def start(copies):
    for copy in copies:
        copy.start()
    return copies


def wait_recv(copies):
    for copy in copies:
        copy.wait_recv()


def wait_send(copies):
    for copy in copies:
        copy.wait_send()


def iota(shape, axis):
    return lax.broadcasted_iota(jnp.int32, shape, axis)


def spread(field, out, p, keep=None):
    moved = pltpu.roll(field[p].astype(F32), 64, 1)
    if keep is not None:
        moved = jnp.where(keep, moved, 0.0)
    lane = iota((16, 128), 1)
    line = iota((16, 128), 0)
    base = p * PLANE if isinstance(p, int) else pl.multiple_of(p * PLANE, PLANE)
    for chunk in range(33):
        if chunk == 0:
            cells = jnp.where(lane >= 64, moved[:, 0:128], 0.0)
        elif chunk == 32:
            cells = jnp.where(lane < 64, moved[:, 0:128], 0.0)
        else:
            cells = moved[:, 128 * chunk : 128 * chunk + 128]
        above = jnp.where(line > 0, pltpu.roll(cells, 1, 0), 0.0)
        below = jnp.where(line < 15, pltpu.roll(cells, 15, 0), 0.0)
        for ky, part in enumerate((above, cells, below)):
            part = part.astype(BF16)
            if chunk < 32:
                out[pl.ds(base + 16 * chunk, 16), 256 * ky : 256 * ky + 128] = part
            if chunk > 0:
                out[pl.ds(base + 16 * (chunk - 1), 16), 256 * ky + 128 : 256 * ky + 256] = part


def turn(field, out, p):
    plane = field[p]
    stacked = jnp.concatenate([plane[:, 128 * g : 128 * g + 128] for g in range(32)], axis=0)
    out[pl.ds((p - 1) * 128, 128), :] = stacked.T


def kernel_gradient(turned, spread_cot, total, planes):
    for p in planes:
        low, high = max(0, 2 - p), min(2, 5 - p)
        first, count = p - 2 + low, high - low + 1
        term = jnp.dot(
            turned[first * 128 : (first + count) * 128, :],
            spread_cot[p * PLANE : (p + 1) * PLANE, :],
            preferred_element_type=F32,
        )
        if p == 2:
            total[...] = term
        else:
            total[low * 128 : (high + 1) * 128, :] += term


def fold(total, flat):
    for kz in range(3):
        for ky in range(3):
            at = 256 * (2 - ky)
            left = total[kz * 128 : kz * 128 + 64, at : at + 256]
            right = total[kz * 128 + 64 : kz * 128 + 128, at : at + 256]
            both = left + pltpu.roll(right, 192, 1)
            row = (kz * 3 + ky) * 3 * 64
            flat[row : row + 64, :] = both[:, 128:256]
            flat[row + 64 : row + 128, :] = pltpu.roll(both[:, 0:128], 64, 1)
            flat[row + 128 : row + 192, :] = both[:, 0:128]


def to_shares(flat, shares):
    lane = iota((32, 128), 1)
    for zh in range(2):
        source = [flat[pl.ds(27 * zh + r, 32, stride=54), :] for r in range(27)]
        for s in range(8):
            halves = [jnp.zeros((32, 128), F32), jnp.zeros((32, 128), F32)]
            for r in range(SHARE * s // 64, (SHARE * s + SHARE - 1) // 64 + 1):
                at = 64 * r - SHARE * s
                moved = pltpu.roll(source[r], at % 128, 1) if at % 128 else source[r]
                low, high = max(at, 0), min(at + 64, SHARE)
                for h in range(2):
                    begin, end = max(low - 128 * h, 0), min(high - 128 * h, 128)
                    if begin < end:
                        halves[h] = jnp.where((lane >= begin) & (lane < end), moved, halves[h])
            for h in range(2):
                shares[s % 2, zh * 4 + s // 2, :, 128 * h : 128 * h + 128] = halves[h]


def from_shares(shares, flat):
    lane = iota((32, 128), 1)
    for zh in range(2):
        source = [
            [shares[s % 2, zh * 4 + s // 2, :, 128 * h : 128 * h + 128].astype(F32) for h in range(2)]
            for s in range(8)
        ]
        for r in range(27):
            out = jnp.zeros((32, 128), F32)
            for s in range(64 * r // SHARE, (64 * r + 63) // SHARE + 1):
                shift = SHARE * s - 64 * r
                low, high = max(64 * r, SHARE * s) - SHARE * s, min(64 * r + 64, SHARE * (s + 1)) - SHARE * s
                for h in range(2):
                    begin, end = max(low, 128 * h), min(high, 128 * h + 128)
                    if begin < end:
                        by = (shift + 128 * h) % 128
                        moved = pltpu.roll(source[s][h], by, 1) if by else source[s][h]
                        out = jnp.where((lane >= begin + shift) & (lane < end + shift), moved, out)
            flat[pl.ds(27 * zh + r, 32, stride=54), :] = out


def bands(flat, forward, backward):
    for kz in range(3):
        for ky in range(3):
            row = (kz * 3 + ky) * 3 * 64
            taps = [flat[row + 64 * kx : row + 64 * kx + 64, :] for kx in range(3)]
            moved = [pltpu.roll(tap, 64, 1) for tap in taps]
            at = kz * 768 + ky * 256
            blocks = (taps[0], taps[1] + moved[0], taps[2] + moved[1], moved[2])
            forward[at : at + 256, :] = jnp.concatenate(blocks, axis=0).astype(BF16)
            at = (2 - kz) * 768 + (2 - ky) * 256
            left = jnp.concatenate([taps[2] + moved[1], moved[2]], axis=0)
            right = jnp.concatenate([taps[0], taps[1] + moved[0]], axis=0)
            backward[at : at + 128, :] = left.T.astype(BF16)
            backward[at + 128 : at + 256, :] = right.T.astype(BF16)


def convolve(spread_field, band, out, z):
    total = None
    for kz in range(3):
        at = (z + kz) * PLANE if isinstance(z, int) else pl.multiple_of((z + kz) * PLANE, PLANE)
        term = jnp.dot(
            spread_field[pl.ds(at, PLANE), :],
            band[kz * 768 : kz * 768 + 768, :],
            preferred_element_type=F32,
        )
        total = term if total is None else total + term
    rounded = total.astype(BF16)
    for g in range(32):
        out[z, :, 128 * g : 128 * g + 128] = rounded[16 * g : 16 * g + 16, :]


def step_kernel(
    act, cot, par, result, input_grad, grad,
    act_pad, cot_pad, share, row, rows, wide,
    a3, b3, turned, total, flat, forward, backward,
    shares, got, mine, sent, parts, terms, term_parts,
    local, hs, gx, gz, gc, rc, rz, rx,
):
    me = place()
    barrier = pltpu.get_barrier_semaphore()
    peers = (
        [xy_peer(me, o) for o in XY]
        + [z_peer(me, d) for d in Z]
        + [core_peer(me), slab_peer(me, 1), slab_peer(me, 7)]
    )
    for peer in peers:
        pl.semaphore_signal(barrier, inc=1, device_id=peer, device_id_type=MESH)
    inner = start([
        pltpu.make_async_copy(cot, cot_pad.at[pl.ds(1, 4)], local.at[0]),
        pltpu.make_async_copy(act, act_pad.at[pl.ds(1, 4)], local.at[1]),
        pltpu.make_async_copy(par, share, local.at[2]),
    ])
    inner[0].wait()

    @pl.loop(1, 5)
    def _(p):
        spread(cot_pad, b3, p)

    inner[1].wait()
    for p in range(1, 5):
        turn(act_pad, turned, p)
    inner[2].wait()
    row[...] = jnp.zeros_like(row)
    row[0, :, 0:SHARE] = share[...]
    rows[me["row"]] = row[0]
    pl.semaphore_wait(barrier, len(peers))

    cot_halo = start([
        remote(cot_pad.at[4], cot_pad.at[0], hs, 0, slab_peer(me, 1)),
        remote(cot_pad.at[1], cot_pad.at[5], hs, 1, slab_peer(me, 7)),
    ])
    own = rows.at[me["row"]]
    gather_xy = start([remote(row.at[0], own, gx, k, xy_peer(me, o)) for k, o in enumerate(XY)])
    act_halo = start([
        remote(act_pad.at[4], act_pad.at[0], hs, 2, slab_peer(me, 1)),
        remote(act_pad.at[1], act_pad.at[5], hs, 3, slab_peer(me, 7)),
    ])

    @pl.loop(1, 5)
    def _(p):
        spread(act_pad, a3, p)

    kernel_gradient(turned, b3, total, (2, 3, 1, 4))

    wait_recv(gather_xy)
    wide[me["core"], me["z"]] = jnp.concatenate([rows[k] for k in range(32)], axis=0).astype(BF16)
    block = wide.at[me["core"], me["z"]]
    gather_z = start([remote(block, block, gz, k, z_peer(me, d)) for k, d in enumerate(Z)])

    def edges(pad, out):
        @pl.loop(0, 2)
        def _(k):
            spread(pad, out, 5 * k, me["slab"] != 7 * k)

    wait_recv(cot_halo)
    edges(cot_pad, b3)
    kernel_gradient(turned, b3, total, (0, 5))
    fold(total, flat)
    to_shares(flat, shares)
    sum_core = start([remote(shares.at[1 - me["core"]], got, rc, 0, core_peer(me))])

    wait_recv(act_halo)
    edges(act_pad, a3)
    wait_recv(sum_core)
    for k in range(8):
        both = shares[me["core"], k] + got[k]
        mine[k] = both
        sent[k] = both.astype(BF16)
    sum_z = start([remote(sent.at[(me["z"] + d) % 8], parts.at[k], rz, k, z_peer(me, d)) for k, d in enumerate(Z)])

    wait_recv(gather_z)
    half = wide.at[me["core"]]
    gather_core = start([remote(half, half, gc, 0, core_peer(me))])
    wait_recv(gather_core)
    from_shares(wide, flat)
    bands(flat, forward, backward)

    @pl.loop(0, 4)
    def _(z):
        convolve(a3, forward, result, z)

    wait_recv(sum_z)
    summed = mine[me["z"]]
    for k in range(7):
        summed = summed + parts[k].astype(F32)
    for k in range(32):
        terms[k] = summed[k : k + 1, :]
    sum_xy = start([
        remote(terms.at[xy_row(me, o)], term_parts.at[k], rx, k, xy_peer(me, o)) for k, o in enumerate(XY)
    ])

    @pl.loop(0, 4)
    def _(z):
        convolve(b3, backward, input_grad, z)

    wait_recv(sum_xy)
    summed = terms[me["row"]]
    for k in range(31):
        summed = summed + term_parts[k]
    grad[...] = summed
    wait_send(cot_halo + gather_xy + act_halo + gather_z + sum_core + sum_z + gather_core + sum_xy)


def step(act, cot, par):
    vmem, hbm = pl.BlockSpec(memory_space=pltpu.VMEM), pl.BlockSpec(memory_space=pltpu.HBM)
    planes = jax.ShapeDtypeStruct((4, 16, 4096), BF16)
    return pl.pallas_call(
        step_kernel,
        out_shape=(planes, planes, jax.ShapeDtypeStruct((1, 256), F32)),
        in_specs=[hbm] * 3,
        out_specs=(vmem,) * 3,
        scratch_shapes=[
            pltpu.VMEM((6, 16, 4096), BF16),
            pltpu.VMEM((6, 16, 4096), BF16),
            pltpu.VMEM((1, SHARE), F32),
            pltpu.VMEM((1, 1, 256), F32),
            pltpu.VMEM((32, 1, 256), F32),
            pltpu.VMEM((2, 8, 32, 256), BF16),
            pltpu.VMEM((6 * PLANE, 768), BF16),
            pltpu.VMEM((6 * PLANE, 768), BF16),
            pltpu.VMEM((512, 512), BF16),
            pltpu.VMEM((384, 768), F32),
            pltpu.VMEM((1728, 128), F32),
            pltpu.VMEM((2304, 128), BF16),
            pltpu.VMEM((2304, 128), BF16),
            pltpu.VMEM((2, 8, 32, 256), F32),
            pltpu.VMEM((8, 32, 256), F32),
            pltpu.VMEM((8, 32, 256), F32),
            pltpu.VMEM((8, 32, 256), BF16),
            pltpu.VMEM((7, 32, 256), BF16),
            pltpu.VMEM((32, 1, 256), F32),
            pltpu.VMEM((31, 1, 256), F32),
            pltpu.SemaphoreType.DMA((3,)),
            pltpu.SemaphoreType.DMA((2, 4)),
            pltpu.SemaphoreType.DMA((2, 31)),
            pltpu.SemaphoreType.DMA((2, 7)),
            pltpu.SemaphoreType.DMA((2, 1)),
            pltpu.SemaphoreType.DMA((2, 1)),
            pltpu.SemaphoreType.DMA((2, 7)),
            pltpu.SemaphoreType.DMA((2, 31)),
        ],
        compiler_params=pltpu.CompilerParams(
            collective_id=0, has_side_effects=True, vmem_limit_bytes=48 * 2**20
        ),
    )(act, cot, par)


def update_kernel(result, input_grad, grad, par, one, two, result_out, input_grad_out, new_par, new_one, new_two, sems):
    copies = start([
        pltpu.make_async_copy(result, result_out, sems.at[0]),
        pltpu.make_async_copy(input_grad, input_grad_out, sems.at[1]),
    ])
    scaled = grad[:, 0:SHARE] / jnp.sqrt(F32(64 * 32 * 16 * 64))
    first_moment = 0.9 * one[...] + 0.1 * scaled
    second_moment = 0.999 * two[...] + 0.001 * scaled * scaled
    change = 3.0 * (first_moment / (1.0 - 0.9**10)) / (jnp.sqrt(second_moment / (1.0 - 0.999**10)) + 1e-08)
    new_par[...] = par[...] - change
    new_one[...] = first_moment
    new_two[...] = second_moment
    for copy in copies:
        copy.wait()


def update(result, input_grad, grad, par, one, two):
    vmem, hbm = pl.BlockSpec(memory_space=pltpu.VMEM), pl.BlockSpec(memory_space=pltpu.HBM)
    planes = jax.ShapeDtypeStruct((4, 16, 4096), BF16)
    share = jax.ShapeDtypeStruct((1, SHARE), F32)
    return pl.pallas_call(
        update_kernel,
        out_shape=(planes, planes) + (share,) * 3,
        in_specs=[vmem] * 6,
        out_specs=(hbm,) * 2 + (vmem,) * 3,
        scratch_shapes=[pltpu.SemaphoreType.DMA((2,))],
        compiler_params=pltpu.CompilerParams(vmem_limit_bytes=8 * 2**20),
    )(result, input_grad, grad, par, one, two)


def on_device(activations, cotangent, params, moment_one, moment_two):
    par, one, two = (a.reshape(1, SHARE) for a in (params, moment_one, moment_two))
    result, input_grad, grad = step(activations[0], cotangent[0], par)
    result, input_grad, new_par, new_one, new_two = update(result, input_grad, grad, par, one, two)
    return (
        result[None],
        input_grad[None],
        new_par.reshape(SHARE),
        new_one.reshape(SHARE),
        new_two.reshape(SHARE),
    )


def solution(mesh):
    field, share = P("dp", "slab", None, None), P(("slab", "dp"))
    return jax.shard_map(
        on_device,
        mesh=mesh,
        in_specs=(field, field, share, share, share),
        out_specs=(field, field, share, share, share),
        check_vma=False,
    )
```

time: 68.5 us -> 48.7 us (0.71)
  the two profiles are of different devices: /device:TPU:4 before, /device:TPU:1 now
where the time goes in v2:
time: 48.7 us; the launch traced here: 48.4 us
  Pallas kernels  44.3 us (91%)
  local copies, waits for them, and re-layouts  3.42 us (7%)
  between operations  0.67 us (1%)
    pallas_call x1, Pallas kernels, step(): pl.pallas_call(step_kernel, out_shape=(planes, planes, jax.ShapeDtypeStru...  42.8 us
    unnamed x10, local copies, waits for them, and re-layouts  3.42 us
    pallas_call x1, Pallas kernels, update(): pl.pallas_call(update_kernel, out_shape=(planes, planes) + (share,) * 3,...  1.55 us

profile of v2, /device:TPU:1, one launch (start us, length us, event | category | flops | bytes accessed | tf_op | source)
XLA Modules:
  0.0 48.4 jit_solution(3562741010529290510)
XLA Ops:
  0.6 0.0 copy-start.2
  0.6 0.7 %copy-done.2 = f32[216]{0:T(256)S(1)} copy-done((f32[216]{0:T(256)S(1)}, f32[216]{0:T(256)}, u32[]{:S(2)}) %copy-start.2) | copy-done | bytes 888
  1.3 0.0 copy-start
  1.3 1.0 %copy-done = bf16[1,4,16,4096]{3,2,1,0:T(8,128)(2,1)S(1)} copy-done((bf16[1,4,16,4096]{3,2,1,0:T(8,128)(2,1)S(1)}, bf16[1,4,16,4096]{3,2,1,0:T(8,128)(2,1)}, u32[]{:S(2)}) %copy-start) | copy-done | bytes 524312
  2.4 0.0 copy-start.1
  2.4 1.0 %copy-done.1 = bf16[1,4,16,4096]{3,2,1,0:T(8,128)(2,1)S(1)} copy-done((bf16[1,4,16,4096]{3,2,1,0:T(8,128)(2,1)S(1)}, bf16[1,4,16,4096]{3,2,1,0:T(8,128)(2,1)}, u32[]{:S(2)}) %copy-start.1) | copy-done | bytes 524312
  3.4 0.0 copy-start.4
  3.4 42.8 %shard_map.92 = (bf16[4,16,4096]{2,1,0:T(8,128)(2,1)S(1)}, bf16[4,16,4096]{2,1,0:T(8,128)(2,1)S(1)}, f32[1,256]{1,0:T(1,128)S(1)}) custom-call(bf16[4,16,4096]{2,1,0:T(8,128)(2,1)S(1)} %bitcast.10, bf16[4,16,4096]{2,1,0:T(8,128)(2,1)S(1)} %bitcast.11, f32[1,216]{1,0:T(1,128)S(1)} %bitcast.12), custom_call_target="tpu_custom_call" | custom-call | tf_op jit(solution)/shard_map/pallas_call | solution.py:335
  46.2 0.0 copy-start.3
  46.2 0.0 copy-done.4
  46.2 0.7 %copy-done.3 = f32[216]{0:T(256)S(1)} copy-done((f32[216]{0:T(256)S(1)}, f32[216]{0:T(256)}, u32[]{:S(2)}) %copy-start.3) | copy-done | bytes 888
  46.9 1.6 %shard_map.93 = (bf16[4,16,4096]{2,1,0:T(8,128)(2,1)}, bf16[4,16,4096]{2,1,0:T(8,128)(2,1)}, f32[1,216]{1,0:T(1,128)}, f32[1,216]{1,0:T(1,128)}, f32[1,216]{1,0:T(1,128)}) custom-call(bf16[4,16,4096]{2,1,0:T(8,128)(2,1)S(1)} %get-tuple-element.13.result, bf16[4,16,4096]{2,1,0:T(8,128)(2,1)S(1)} %get-tuple-element.14.input_grad, ...), custom_call_target="tpu_custom_call" | custom-call | tf_op jit(solution)/shard_map/pallas_call | solution.py:396
Async XLA Ops:
  0.6 0.7 %copy-start.2 = (f32[216]{0:T(256)S(1)}, f32[216]{0:T(256)}, u32[]{:S(2)}) copy-start(f32[216]{0:T(256)} %param.7) | copy-start | bytes 2596
  1.3 1.0 %copy-start = (bf16[1,4,16,4096]{3,2,1,0:T(8,128)(2,1)S(1)}, bf16[1,4,16,4096]{3,2,1,0:T(8,128)(2,1)}, u32[]{:S(2)}) copy-start(bf16[1,4,16,4096]{3,2,1,0:T(8,128)(2,1)} %param.5) | copy-start | bytes 1572868
  2.4 1.0 %copy-start.1 = (bf16[1,4,16,4096]{3,2,1,0:T(8,128)(2,1)S(1)}, bf16[1,4,16,4096]{3,2,1,0:T(8,128)(2,1)}, u32[]{:S(2)}) copy-start(bf16[1,4,16,4096]{3,2,1,0:T(8,128)(2,1)} %param.6) | copy-start | bytes 1572868
  3.4 42.8 %copy-start.4 = (f32[216]{0:T(256)S(1)}, f32[216]{0:T(256)}, u32[]{:S(2)}) copy-start(f32[216]{0:T(256)} %param.9) | copy-start | bytes 2596
  46.2 0.7 %copy-start.3 = (f32[216]{0:T(256)S(1)}, f32[216]{0:T(256)}, u32[]{:S(2)}) copy-start(f32[216]{0:T(256)} %param.8) | copy-start | bytes 2596

commit v3 on v2

--- a/solution.py
+++ b/solution.py
@@ -10,6 +10,7 @@
 BF16 = jnp.bfloat16
 SHARE = 216
 PLANE = 512
+VMEM_MIB = 52.5
 
 
 def place():
@@ -33,12 +34,20 @@
     [(dx, dy) for dx in range(4) for dy in range(8) if dx or dy],
     key=lambda o: -(hops(o[0], 4) + hops(o[1], 8)),
 )
-Z = sorted(range(1, 8), key=lambda d: -hops(d, 8))
+X, EIGHT = (2, 1, 3), sorted(range(1, 8), key=lambda d: -hops(d, 8))
 
 
 def xy_peer(me, offset):
     x, y = (me["x"] + offset[0]) % 4, (me["y"] + offset[1]) % 8
     return ((y % 2) * 4 + x, (y // 2) * 16 + me["dp"] % 16)
+
+
+def x_peer(me, d):
+    return xy_peer(me, (d, 0))
+
+
+def y_peer(me, d):
+    return xy_peer(me, (0, d))
 
 
 def xy_row(me, offset):
@@ -187,114 +196,127 @@
 
 
 def bands(flat, forward, backward):
+    zero = jnp.zeros((256, 128), BF16)
+    for out in (forward, backward):
+        for ky in range(3):
+            out[256 * ky : 256 * ky + 256, 128:256] = zero
+            out[3 * 768 + 256 * ky : 3 * 768 + 256 * ky + 256, 0:128] = zero
     for kz in range(3):
         for ky in range(3):
             row = (kz * 3 + ky) * 3 * 64
             taps = [flat[row + 64 * kx : row + 64 * kx + 64, :] for kx in range(3)]
             moved = [pltpu.roll(tap, 64, 1) for tap in taps]
-            at = kz * 768 + ky * 256
             blocks = (taps[0], taps[1] + moved[0], taps[2] + moved[1], moved[2])
-            forward[at : at + 256, :] = jnp.concatenate(blocks, axis=0).astype(BF16)
-            at = (2 - kz) * 768 + (2 - ky) * 256
+            ahead = jnp.concatenate(blocks, axis=0).astype(BF16)
             left = jnp.concatenate([taps[2] + moved[1], moved[2]], axis=0)
             right = jnp.concatenate([taps[0], taps[1] + moved[0]], axis=0)
-            backward[at : at + 128, :] = left.T.astype(BF16)
-            backward[at + 128 : at + 256, :] = right.T.astype(BF16)
-
-
-def convolve(spread_field, band, out, z):
-    total = None
-    for kz in range(3):
-        at = (z + kz) * PLANE if isinstance(z, int) else pl.multiple_of((z + kz) * PLANE, PLANE)
-        term = jnp.dot(
-            spread_field[pl.ds(at, PLANE), :],
-            band[kz * 768 : kz * 768 + 768, :],
-            preferred_element_type=F32,
-        )
-        total = term if total is None else total + term
-    rounded = total.astype(BF16)
-    for g in range(32):
-        out[z, :, 128 * g : 128 * g + 128] = rounded[16 * g : 16 * g + 16, :]
+            back = jnp.concatenate([left.T, right.T], axis=0).astype(BF16)
+            for plane in range(2):
+                lanes = slice(128 * plane, 128 * plane + 128)
+                at = (kz + plane) * 768 + ky * 256
+                forward[at : at + 256, lanes] = ahead
+                at = (2 - kz + plane) * 768 + (2 - ky) * 256
+                backward[at : at + 256, lanes] = back
+
+
+def convolve(spread_field, band, out):
+    for pair in range(2):
+        at = pair * 2 * PLANE
+        cells = jnp.concatenate([spread_field[at + j * PLANE : at + (j + 1) * PLANE, :] for j in range(4)], axis=1)
+        rounded = jnp.dot(cells, band[...], preferred_element_type=F32).astype(BF16)
+        for plane in range(2):
+            for g in range(32):
+                out[2 * pair + plane, :, 128 * g : 128 * g + 128] = rounded[
+                    16 * g : 16 * g + 16, 128 * plane : 128 * plane + 128
+                ]
 
 
 def step_kernel(
-    act, cot, par, result, input_grad, grad,
+    act, cot, par, one, two, result, input_grad, new_par, new_one, new_two,
     act_pad, cot_pad, share, row, rows, wide,
     a3, b3, turned, total, flat, forward, backward,
     shares, got, mine, sent, parts, terms, term_parts,
-    local, hs, gx, gz, gc, rc, rz, rx,
+    local, hs, gx, gy, gz, gc, rc, rz, rx,
 ):
     me = place()
     barrier = pltpu.get_barrier_semaphore()
     peers = (
-        [xy_peer(me, o) for o in XY]
-        + [z_peer(me, d) for d in Z]
-        + [core_peer(me), slab_peer(me, 1), slab_peer(me, 7)]
+        [z_peer(me, d) for d in EIGHT]
+        + [y_peer(me, d) for d in EIGHT]
+        + [x_peer(me, d) for d in X]
+        + [slab_peer(me, 1), slab_peer(me, 7), core_peer(me)]
     )
+    loads = start([
+        pltpu.make_async_copy(par, share.at[0], local.at[0]),
+        pltpu.make_async_copy(cot, cot_pad.at[pl.ds(1, 4)], local.at[1]),
+        pltpu.make_async_copy(act, act_pad.at[pl.ds(1, 4)], local.at[2]),
+        pltpu.make_async_copy(one, share.at[1], local.at[3]),
+        pltpu.make_async_copy(two, share.at[2], local.at[4]),
+    ])
     for peer in peers:
         pl.semaphore_signal(barrier, inc=1, device_id=peer, device_id_type=MESH)
-    inner = start([
-        pltpu.make_async_copy(cot, cot_pad.at[pl.ds(1, 4)], local.at[0]),
-        pltpu.make_async_copy(act, act_pad.at[pl.ds(1, 4)], local.at[1]),
-        pltpu.make_async_copy(par, share, local.at[2]),
+    row[...] = jnp.zeros_like(row)
+    loads[0].wait()
+    row[0, :, 0:SHARE] = share[0]
+    rows[me["y"], me["x"]] = row[0]
+    pl.semaphore_wait(barrier, len(peers))
+
+    cot_halo = start([
+        remote(cot.at[3], cot_pad.at[0], hs, 0, slab_peer(me, 1)),
+        remote(cot.at[0], cot_pad.at[5], hs, 1, slab_peer(me, 7)),
     ])
-    inner[0].wait()
-
-    @pl.loop(1, 5)
-    def _(p):
-        spread(cot_pad, b3, p)
-
-    inner[1].wait()
-    for p in range(1, 5):
-        turn(act_pad, turned, p)
-    inner[2].wait()
-    row[...] = jnp.zeros_like(row)
-    row[0, :, 0:SHARE] = share[...]
-    rows[me["row"]] = row[0]
-    pl.semaphore_wait(barrier, len(peers))
-
-    cot_halo = start([
-        remote(cot_pad.at[4], cot_pad.at[0], hs, 0, slab_peer(me, 1)),
-        remote(cot_pad.at[1], cot_pad.at[5], hs, 1, slab_peer(me, 7)),
-    ])
-    own = rows.at[me["row"]]
-    gather_xy = start([remote(row.at[0], own, gx, k, xy_peer(me, o)) for k, o in enumerate(XY)])
-    act_halo = start([
-        remote(act_pad.at[4], act_pad.at[0], hs, 2, slab_peer(me, 1)),
-        remote(act_pad.at[1], act_pad.at[5], hs, 3, slab_peer(me, 7)),
-    ])
-
-    @pl.loop(1, 5)
-    def _(p):
-        spread(act_pad, a3, p)
-
-    kernel_gradient(turned, b3, total, (2, 3, 1, 4))
-
-    wait_recv(gather_xy)
-    wide[me["core"], me["z"]] = jnp.concatenate([rows[k] for k in range(32)], axis=0).astype(BF16)
-    block = wide.at[me["core"], me["z"]]
-    gather_z = start([remote(block, block, gz, k, z_peer(me, d)) for k, d in enumerate(Z)])
+    own = rows.at[me["y"], me["x"]]
+    gather_x = start([remote(row.at[0], own, gx, k, x_peer(me, d)) for k, d in enumerate(X)])
+
+    def inner(pad, out):
+        @pl.loop(1, 5)
+        def _(p):
+            spread(pad, out, p)
 
     def edges(pad, out):
         @pl.loop(0, 2)
         def _(k):
             spread(pad, out, 5 * k, me["slab"] != 7 * k)
 
+    loads[1].wait()
+    inner(cot_pad, b3)
+    loads[2].wait()
+    for p in range(1, 5):
+        turn(act_pad, turned, p)
+    kernel_gradient(turned, b3, total, (2, 3, 1, 4))
+    wait_recv(gather_x)
+    four = rows.at[me["y"]]
+    gather_y = start([remote(four, four, gy, k, y_peer(me, d)) for k, d in enumerate(EIGHT)])
+    inner(act_pad, a3)
+    loads[3].wait()
+    loads[4].wait()
+
     wait_recv(cot_halo)
+    act_halo = start([
+        remote(act.at[3], act_pad.at[0], hs, 2, slab_peer(me, 1)),
+        remote(act.at[0], act_pad.at[5], hs, 3, slab_peer(me, 7)),
+    ])
     edges(cot_pad, b3)
     kernel_gradient(turned, b3, total, (0, 5))
     fold(total, flat)
     to_shares(flat, shares)
     sum_core = start([remote(shares.at[1 - me["core"]], got, rc, 0, core_peer(me))])
 
-    wait_recv(act_halo)
-    edges(act_pad, a3)
+    wait_recv(gather_y)
+    wide[me["core"], me["z"]] = jnp.concatenate(
+        [rows[(k % 4) * 2 + k // 16, (k // 4) % 4] for k in range(32)], axis=0
+    ).astype(BF16)
+    block = wide.at[me["core"], me["z"]]
+    gather_z = start([remote(block, block, gz, k, z_peer(me, d)) for k, d in enumerate(EIGHT)])
+
     wait_recv(sum_core)
     for k in range(8):
         both = shares[me["core"], k] + got[k]
         mine[k] = both
         sent[k] = both.astype(BF16)
-    sum_z = start([remote(sent.at[(me["z"] + d) % 8], parts.at[k], rz, k, z_peer(me, d)) for k, d in enumerate(Z)])
+    sum_z = start([remote(sent.at[(me["z"] + d) % 8], parts.at[k], rz, k, z_peer(me, d)) for k, d in enumerate(EIGHT)])
+    wait_recv(act_halo)
+    edges(act_pad, a3)
 
     wait_recv(gather_z)
     half = wide.at[me["core"]]
@@ -302,10 +324,6 @@
     wait_recv(gather_core)
     from_shares(wide, flat)
     bands(flat, forward, backward)
-
-    @pl.loop(0, 4)
-    def _(z):
-        convolve(a3, forward, result, z)
 
     wait_recv(sum_z)
     summed = mine[me["z"]]
@@ -317,40 +335,46 @@
         remote(terms.at[xy_row(me, o)], term_parts.at[k], rx, k, xy_peer(me, o)) for k, o in enumerate(XY)
     ])
 
-    @pl.loop(0, 4)
-    def _(z):
-        convolve(b3, backward, input_grad, z)
+    convolve(a3, forward, result)
+    convolve(b3, backward, input_grad)
 
     wait_recv(sum_xy)
     summed = terms[me["row"]]
     for k in range(31):
         summed = summed + term_parts[k]
-    grad[...] = summed
-    wait_send(cot_halo + gather_xy + act_halo + gather_z + sum_core + sum_z + gather_core + sum_xy)
-
-
-def step(act, cot, par):
+    scaled = summed[:, 0:SHARE] / jnp.sqrt(F32(64 * 32 * 16 * 64))
+    first_moment = 0.9 * share[1] + 0.1 * scaled
+    second_moment = 0.999 * share[2] + 0.001 * scaled * scaled
+    change = 3.0 * (first_moment / (1.0 - 0.9**10)) / (jnp.sqrt(second_moment / (1.0 - 0.999**10)) + 1e-08)
+    new_par[...] = share[0] - change
+    new_one[...] = first_moment
+    new_two[...] = second_moment
+    wait_send(cot_halo + gather_x + gather_y + act_halo + gather_z + sum_core + sum_z + gather_core + sum_xy)
+
+
+def step(act, cot, par, one, two):
     vmem, hbm = pl.BlockSpec(memory_space=pltpu.VMEM), pl.BlockSpec(memory_space=pltpu.HBM)
     planes = jax.ShapeDtypeStruct((4, 16, 4096), BF16)
+    share = jax.ShapeDtypeStruct((1, SHARE), F32)
     return pl.pallas_call(
         step_kernel,
-        out_shape=(planes, planes, jax.ShapeDtypeStruct((1, 256), F32)),
-        in_specs=[hbm] * 3,
-        out_specs=(vmem,) * 3,
+        out_shape=(planes, planes) + (share,) * 3,
+        in_specs=[hbm] * 5,
+        out_specs=(vmem,) * 5,
         scratch_shapes=[
             pltpu.VMEM((6, 16, 4096), BF16),
             pltpu.VMEM((6, 16, 4096), BF16),
-            pltpu.VMEM((1, SHARE), F32),
+            pltpu.VMEM((3, 1, SHARE), F32),
             pltpu.VMEM((1, 1, 256), F32),
-            pltpu.VMEM((32, 1, 256), F32),
+            pltpu.VMEM((8, 4, 1, 256), F32),
             pltpu.VMEM((2, 8, 32, 256), BF16),
             pltpu.VMEM((6 * PLANE, 768), BF16),
             pltpu.VMEM((6 * PLANE, 768), BF16),
             pltpu.VMEM((512, 512), BF16),
             pltpu.VMEM((384, 768), F32),
             pltpu.VMEM((1728, 128), F32),
-            pltpu.VMEM((2304, 128), BF16),
-            pltpu.VMEM((2304, 128), BF16),
+            pltpu.VMEM((3072, 256), BF16),
+            pltpu.VMEM((3072, 256), BF16),
             pltpu.VMEM((2, 8, 32, 256), F32),
             pltpu.VMEM((8, 32, 256), F32),
             pltpu.VMEM((8, 32, 256), F32),
@@ -358,9 +382,10 @@
             pltpu.VMEM((7, 32, 256), BF16),
             pltpu.VMEM((32, 1, 256), F32),
             pltpu.VMEM((31, 1, 256), F32),
-            pltpu.SemaphoreType.DMA((3,)),
+            pltpu.SemaphoreType.DMA((5,)),
             pltpu.SemaphoreType.DMA((2, 4)),
-            pltpu.SemaphoreType.DMA((2, 31)),
+            pltpu.SemaphoreType.DMA((2, 3)),
+            pltpu.SemaphoreType.DMA((2, 7)),
             pltpu.SemaphoreType.DMA((2, 7)),
             pltpu.SemaphoreType.DMA((2, 1)),
             pltpu.SemaphoreType.DMA((2, 1)),
@@ -368,45 +393,34 @@
             pltpu.SemaphoreType.DMA((2, 31)),
         ],
         compiler_params=pltpu.CompilerParams(
-            collective_id=0, has_side_effects=True, vmem_limit_bytes=48 * 2**20
+            collective_id=0, has_side_effects=True, vmem_limit_bytes=int(VMEM_MIB * 2**20)
         ),
-    )(act, cot, par)
-
-
-def update_kernel(result, input_grad, grad, par, one, two, result_out, input_grad_out, new_par, new_one, new_two, sems):
-    copies = start([
-        pltpu.make_async_copy(result, result_out, sems.at[0]),
-        pltpu.make_async_copy(input_grad, input_grad_out, sems.at[1]),
-    ])
-    scaled = grad[:, 0:SHARE] / jnp.sqrt(F32(64 * 32 * 16 * 64))
-    first_moment = 0.9 * one[...] + 0.1 * scaled
-    second_moment = 0.999 * two[...] + 0.001 * scaled * scaled
-    change = 3.0 * (first_moment / (1.0 - 0.9**10)) / (jnp.sqrt(second_moment / (1.0 - 0.999**10)) + 1e-08)
-    new_par[...] = par[...] - change
-    new_one[...] = first_moment
-    new_two[...] = second_moment
+    )(act, cot, par, one, two)
+
+
+def place_kernel(*refs):
+    sems = refs[-1]
+    copies = start([pltpu.make_async_copy(refs[k], refs[k + 5], sems.at[k]) for k in range(5)])
     for copy in copies:
         copy.wait()
 
 
-def update(result, input_grad, grad, par, one, two):
-    vmem, hbm = pl.BlockSpec(memory_space=pltpu.VMEM), pl.BlockSpec(memory_space=pltpu.HBM)
-    planes = jax.ShapeDtypeStruct((4, 16, 4096), BF16)
-    share = jax.ShapeDtypeStruct((1, SHARE), F32)
+def place_outputs(*arrays):
+    hbm = pl.BlockSpec(memory_space=pltpu.HBM)
     return pl.pallas_call(
-        update_kernel,
-        out_shape=(planes, planes) + (share,) * 3,
-        in_specs=[vmem] * 6,
-        out_specs=(hbm,) * 2 + (vmem,) * 3,
-        scratch_shapes=[pltpu.SemaphoreType.DMA((2,))],
+        place_kernel,
+        out_shape=tuple(jax.ShapeDtypeStruct(a.shape, a.dtype) for a in arrays),
+        in_specs=[hbm] * 5,
+        out_specs=(hbm,) * 5,
+        scratch_shapes=[pltpu.SemaphoreType.DMA((5,))],
         compiler_params=pltpu.CompilerParams(vmem_limit_bytes=8 * 2**20),
-    )(result, input_grad, grad, par, one, two)
+    )(*arrays)
 
 
 def on_device(activations, cotangent, params, moment_one, moment_two):
     par, one, two = (a.reshape(1, SHARE) for a in (params, moment_one, moment_two))
-    result, input_grad, grad = step(activations[0], cotangent[0], par)
-    result, input_grad, new_par, new_one, new_two = update(result, input_grad, grad, par, one, two)
+    outputs = step(activations[0], cotangent[0], par, one, two)
+    result, input_grad, new_par, new_one, new_two = place_outputs(*outputs)
     return (
         result[None],
         input_grad[None],

time: 48.7 us -> 41.5 us (0.85)
  Pallas kernels: 44.3 us -> 40 us
  local copies, waits for them, and re-layouts: 3.42 us -> 0.69 us
    pallas_call x2, Pallas kernels: 44.3 us -> 40 us  [the longest x1 39 us: step(): pl.pallas_call(step_kernel, out_shape=(planes, planes) + (share,) * 3, in...]
    unnamed x10 -> x6, local copies, waits for them, and re-layouts: 3.42 us -> 0.69 us
where the time goes in v3:
time: 41.5 us; the launch traced here: 41.4 us
  Pallas kernels  40 us (96%)
  local copies, waits for them, and re-layouts  0.69 us (2%)
  between operations  0.67 us (2%)
    pallas_call x1, Pallas kernels, step(): pl.pallas_call(step_kernel, out_shape=(planes, planes) + (share,) * 3, in...  39 us
    pallas_call x1, Pallas kernels, place_outputs(): pl.pallas_call(place_kernel, out_shape=tuple((jax.ShapeDtypeStruct(a.shap...  1.02 us

profile of v3, /device:TPU:1, one launch (start us, length us, event | category | flops | bytes accessed | tf_op | source)
XLA Modules:
  0.0 41.4 jit_solution(12529246787625271786)
XLA Ops:
  0.6 0.0 copy-start.1
  0.6 0.0 copy-start.2
  0.7 0.0 copy-start
  0.7 0.7 %copy-done.1 = f32[216]{0:T(256)S(1)} copy-done((f32[216]{0:T(256)S(1)}, f32[216]{0:T(256)}, u32[]{:S(2)}) %copy-start.1) | copy-done | bytes 888
  1.3 0.0 copy-done.2
  1.3 0.0 copy-done
  1.3 39.0 %shard_map.92 = (bf16[4,16,4096]{2,1,0:T(8,128)(2,1)S(1)}, bf16[4,16,4096]{2,1,0:T(8,128)(2,1)S(1)}, f32[1,216]{1,0:T(1,128)S(1)}, f32[1,216]{1,0:T(1,128)S(1)}, f32[1,216]{1,0:T(1,128)S(1)}) custom-call(bf16[4,16,4096]{2,1,0:T(8,128)(2,1)} %bitcast.13, bf16[4,16,4096]{2,1,0:T(8,128)(2,1)} %bitcast.14, f32[1,216]{1,0:T(1,128)S(1)} %bitcast.10, ...), custom_call_target="tpu_custom_call" | custom-call | tf_op jit(solution)/shard_map/pallas_call | solution.py:359
  40.4 1.0 %shard_map.93 = (bf16[4,16,4096]{2,1,0:T(8,128)(2,1)}, bf16[4,16,4096]{2,1,0:T(8,128)(2,1)}, f32[1,216]{1,0:T(1,128)}, f32[1,216]{1,0:T(1,128)}, f32[1,216]{1,0:T(1,128)}) custom-call(bf16[4,16,4096]{2,1,0:T(8,128)(2,1)S(1)} %get-tuple-element.15.refs_0_, bf16[4,16,4096]{2,1,0:T(8,128)(2,1)S(1)} %get-tuple-element.16.refs_1_, ...), custom_call_target="tpu_custom_call" | custom-call | tf_op jit(solution)/shard_map/pallas_call | solution.py:410
Async XLA Ops:
  0.6 0.7 %copy-start.1 = (f32[216]{0:T(256)S(1)}, f32[216]{0:T(256)}, u32[]{:S(2)}) copy-start(f32[216]{0:T(256)} %param.8) | copy-start | bytes 2596
  0.6 0.7 %copy-start.2 = (f32[216]{0:T(256)S(1)}, f32[216]{0:T(256)}, u32[]{:S(2)}) copy-start(f32[216]{0:T(256)} %param.9) | copy-start | bytes 2596
  0.7 0.7 %copy-start = (f32[216]{0:T(256)S(1)}, f32[216]{0:T(256)}, u32[]{:S(2)}) copy-start(f32[216]{0:T(256)} %param.7) | copy-start | bytes 2596

commit v4 on v3

--- a/solution.py
+++ b/solution.py
@@ -22,6 +22,7 @@
         "y": (dp // 16) * 2 + slab // 4,
         "row": slab * 4 + dp // 16,
         "z": (dp // 2) % 8,
+        "z_row": ((dp // 2) % 4) * 2 + (dp // 8) % 2,
         "core": dp % 2,
     }
 
@@ -143,8 +144,8 @@
             total[low * 128 : (high + 1) * 128, :] += term
 
 
-def fold(total, flat):
-    for kz in range(3):
+def fold(total, flat, planes):
+    for kz in planes:
         for ky in range(3):
             at = 256 * (2 - ky)
             left = total[kz * 128 : kz * 128 + 64, at : at + 256]
@@ -175,24 +176,27 @@
 
 
 def from_shares(shares, flat):
-    lane = iota((32, 128), 1)
-    for zh in range(2):
-        source = [
-            [shares[s % 2, zh * 4 + s // 2, :, 128 * h : 128 * h + 128].astype(F32) for h in range(2)]
-            for s in range(8)
-        ]
-        for r in range(27):
-            out = jnp.zeros((32, 128), F32)
-            for s in range(64 * r // SHARE, (64 * r + 63) // SHARE + 1):
-                shift = SHARE * s - 64 * r
-                low, high = max(64 * r, SHARE * s) - SHARE * s, min(64 * r + 64, SHARE * (s + 1)) - SHARE * s
-                for h in range(2):
-                    begin, end = max(low, 128 * h), min(high, 128 * h + 128)
-                    if begin < end:
-                        by = (shift + 128 * h) % 128
-                        moved = pltpu.roll(source[s][h], by, 1) if by else source[s][h]
-                        out = jnp.where((lane >= begin + shift) & (lane < end + shift), moved, out)
-            flat[pl.ds(27 * zh + r, 32, stride=54), :] = out
+    lane = iota((64, 128), 1)
+    source = []
+    for s in range(8):
+        rows = [shares[s % 2, y].astype(F32)[8 * (s // 2) : 8 * (s // 2) + 8, :] for y in range(8)]
+        whole = jnp.concatenate(rows, axis=0)
+        source.append([whole[:, 0:128], whole[:, 128:256]])
+    for r in range(27):
+        out = jnp.zeros((64, 128), F32)
+        for s in range(64 * r // SHARE, (64 * r + 63) // SHARE + 1):
+            shift = SHARE * s - 64 * r
+            low, high = max(64 * r, SHARE * s) - SHARE * s, min(64 * r + 64, SHARE * (s + 1)) - SHARE * s
+            for h in range(2):
+                begin, end = max(low, 128 * h), min(high, 128 * h + 128)
+                if begin < end:
+                    by = (shift + 128 * h) % 128
+                    moved = pltpu.roll(source[s][h], by, 1) if by else source[s][h]
+                    out = jnp.where((lane >= begin + shift) & (lane < end + shift), moved, out)
+        for k in range(16):
+            y, zh = k // 2, k % 2
+            first = 54 * ((y % 2) * 16 + y // 2) + 27 * zh + r
+            flat[pl.ds(first, 4, stride=216), :] = out[4 * k : 4 * k + 4, :]
 
 
 def bands(flat, forward, backward):
@@ -236,15 +240,16 @@
     act_pad, cot_pad, share, row, rows, wide,
     a3, b3, turned, total, flat, forward, backward,
     shares, got, mine, sent, parts, terms, term_parts,
-    local, hs, gx, gy, gz, gc, rc, rz, rx,
+    local, come, hs, gx, gy, gz, gc, rc, rz, rx,
 ):
     me = place()
     barrier = pltpu.get_barrier_semaphore()
     peers = (
-        [z_peer(me, d) for d in EIGHT]
-        + [y_peer(me, d) for d in EIGHT]
+        [slab_peer(me, 1), slab_peer(me, 7)]
         + [x_peer(me, d) for d in X]
-        + [slab_peer(me, 1), slab_peer(me, 7), core_peer(me)]
+        + [z_peer(me, d) for d in (2, 6, 1, 7)]
+        + [y_peer(me, d) for d in (2, 6, 1, 7)]
+        + [core_peer(me)]
     )
     loads = start([
         pltpu.make_async_copy(par, share.at[0], local.at[0]),
@@ -255,18 +260,14 @@
     ])
     for peer in peers:
         pl.semaphore_signal(barrier, inc=1, device_id=peer, device_id_type=MESH)
-    row[...] = jnp.zeros_like(row)
-    loads[0].wait()
-    row[0, :, 0:SHARE] = share[0]
-    rows[me["y"], me["x"]] = row[0]
-    pl.semaphore_wait(barrier, len(peers))
-
-    cot_halo = start([
-        remote(cot.at[3], cot_pad.at[0], hs, 0, slab_peer(me, 1)),
-        remote(cot.at[0], cot_pad.at[5], hs, 1, slab_peer(me, 7)),
-    ])
-    own = rows.at[me["y"], me["x"]]
-    gather_x = start([remote(row.at[0], own, gx, k, x_peer(me, d)) for k, d in enumerate(X)])
+
+    def greet(axis):
+        for d in (2, 6):
+            peer = (y_peer, z_peer)[axis](me, d)
+            pl.semaphore_signal(come.at[axis], inc=1, device_id=peer, device_id_type=MESH)
+
+    def greeted(axis):
+        pl.semaphore_wait(come.at[axis], 2)
 
     def inner(pad, out):
         @pl.loop(1, 5)
@@ -278,52 +279,60 @@
         def _(k):
             spread(pad, out, 5 * k, me["slab"] != 7 * k)
 
+    row[...] = jnp.zeros_like(row)
+    loads[0].wait()
+    row[0, :, 0:SHARE] = share[0]
+    rows[me["z_row"], me["x"]] = row[0]
     loads[1].wait()
     inner(cot_pad, b3)
     loads[2].wait()
     for p in range(1, 5):
         turn(act_pad, turned, p)
+    pl.semaphore_wait(barrier, len(peers))
+
+    greet(1)
+    cot_halo = start([
+        remote(cot_pad.at[4], cot_pad.at[0], hs, 0, slab_peer(me, 1)),
+        remote(cot_pad.at[1], cot_pad.at[5], hs, 1, slab_peer(me, 7)),
+    ])
+    own = rows.at[me["z_row"], me["x"]]
+    gather_x = start([remote(row.at[0], own, gx, k, x_peer(me, d)) for k, d in enumerate(X)])
     kernel_gradient(turned, b3, total, (2, 3, 1, 4))
+    fold(total, flat, (1,))
     wait_recv(gather_x)
-    four = rows.at[me["y"]]
-    gather_y = start([remote(four, four, gy, k, y_peer(me, d)) for k, d in enumerate(EIGHT)])
+    greet(0)
+    greeted(1)
+    four = rows.at[me["z_row"]]
+    gather_z = start([remote(four, four, gz, k, z_peer(me, d)) for k, d in enumerate(EIGHT)])
     inner(act_pad, a3)
     loads[3].wait()
     loads[4].wait()
-
     wait_recv(cot_halo)
     act_halo = start([
-        remote(act.at[3], act_pad.at[0], hs, 2, slab_peer(me, 1)),
-        remote(act.at[0], act_pad.at[5], hs, 3, slab_peer(me, 7)),
+        remote(act_pad.at[4], act_pad.at[0], hs, 2, slab_peer(me, 1)),
+        remote(act_pad.at[1], act_pad.at[5], hs, 3, slab_peer(me, 7)),
     ])
     edges(cot_pad, b3)
     kernel_gradient(turned, b3, total, (0, 5))
-    fold(total, flat)
+    fold(total, flat, (0, 2))
     to_shares(flat, shares)
     sum_core = start([remote(shares.at[1 - me["core"]], got, rc, 0, core_peer(me))])
-
-    wait_recv(gather_y)
-    wide[me["core"], me["z"]] = jnp.concatenate(
-        [rows[(k % 4) * 2 + k // 16, (k // 4) % 4] for k in range(32)], axis=0
-    ).astype(BF16)
-    block = wide.at[me["core"], me["z"]]
-    gather_z = start([remote(block, block, gz, k, z_peer(me, d)) for k, d in enumerate(EIGHT)])
-
     wait_recv(sum_core)
     for k in range(8):
         both = shares[me["core"], k] + got[k]
         mine[k] = both
         sent[k] = both.astype(BF16)
-    sum_z = start([remote(sent.at[(me["z"] + d) % 8], parts.at[k], rz, k, z_peer(me, d)) for k, d in enumerate(EIGHT)])
+    sum_z = start([
+        remote(sent.at[(me["z"] + d) % 8], parts.at[k], rz, k, z_peer(me, d)) for k, d in enumerate(EIGHT)
+    ])
+
+    greeted(0)
+    wait_recv(gather_z)
+    wide[me["core"], me["y"]] = jnp.concatenate([rows[k // 4, k % 4] for k in range(32)], axis=0).astype(BF16)
+    block = wide.at[me["core"], me["y"]]
+    gather_y = start([remote(block, block, gy, k, y_peer(me, d)) for k, d in enumerate(EIGHT)])
     wait_recv(act_halo)
     edges(act_pad, a3)
-
-    wait_recv(gather_z)
-    half = wide.at[me["core"]]
-    gather_core = start([remote(half, half, gc, 0, core_peer(me))])
-    wait_recv(gather_core)
-    from_shares(wide, flat)
-    bands(flat, forward, backward)
 
     wait_recv(sum_z)
     summed = mine[me["z"]]
@@ -331,14 +340,20 @@
         summed = summed + parts[k].astype(F32)
     for k in range(32):
         terms[k] = summed[k : k + 1, :]
-    sum_xy = start([
-        remote(terms.at[xy_row(me, o)], term_parts.at[k], rx, k, xy_peer(me, o)) for k, o in enumerate(XY)
-    ])
-
+    sum_xy = [remote(terms.at[xy_row(me, o)], term_parts.at[k], rx, 0, xy_peer(me, o)) for k, o in enumerate(XY)]
+    start(sum_xy)
+    all_xy = remote(term_parts, term_parts, rx, 0, xy_peer(me, XY[0]))
+    wait_recv(gather_y)
+    half = wide.at[me["core"]]
+    gather_core = start([remote(half, half, gc, 0, core_peer(me))])
+    wait_recv(gather_core)
+    from_shares(wide, flat)
+    bands(flat, forward, backward)
     convolve(a3, forward, result)
     convolve(b3, backward, input_grad)
 
-    wait_recv(sum_xy)
+    wait_send(cot_halo + gather_x + gather_y + act_halo + gather_z + sum_core + sum_z + gather_core)
+    wait_recv([all_xy])
     summed = terms[me["row"]]
     for k in range(31):
         summed = summed + term_parts[k]
@@ -349,7 +364,7 @@
     new_par[...] = share[0] - change
     new_one[...] = first_moment
     new_two[...] = second_moment
-    wait_send(cot_halo + gather_x + gather_y + act_halo + gather_z + sum_core + sum_z + gather_core + sum_xy)
+    wait_send([all_xy])
 
 
 def step(act, cot, par, one, two):
@@ -383,6 +398,7 @@
             pltpu.VMEM((32, 1, 256), F32),
             pltpu.VMEM((31, 1, 256), F32),
             pltpu.SemaphoreType.DMA((5,)),
+            pltpu.SemaphoreType.REGULAR((2,)),
             pltpu.SemaphoreType.DMA((2, 4)),
             pltpu.SemaphoreType.DMA((2, 3)),
             pltpu.SemaphoreType.DMA((2, 7)),
@@ -390,7 +406,7 @@
             pltpu.SemaphoreType.DMA((2, 1)),
             pltpu.SemaphoreType.DMA((2, 1)),
             pltpu.SemaphoreType.DMA((2, 7)),
-            pltpu.SemaphoreType.DMA((2, 31)),
+            pltpu.SemaphoreType.DMA((2, 1)),
         ],
         compiler_params=pltpu.CompilerParams(
             collective_id=0, has_side_effects=True, vmem_limit_bytes=int(VMEM_MIB * 2**20)

time: 41.5 us -> 37.5 us (0.904)
  Pallas kernels: 40 us -> 36 us
    pallas_call x1, Pallas kernels: 39 us -> 34.9 us  [step(): pl.pallas_call(step_kernel, out_shape=(planes, planes) + (share,) * 3, in...]
where the time goes in v4:
time: 37.5 us; the launch traced here: 37.3 us
  Pallas kernels  36 us (96%)
  local copies, waits for them, and re-layouts  0.69 us (2%)
  between operations  0.67 us (2%)
    pallas_call x1, Pallas kernels, step(): pl.pallas_call(step_kernel, out_shape=(planes, planes) + (share,) * 3, in...  34.9 us
    pallas_call x1, Pallas kernels, place_outputs(): pl.pallas_call(place_kernel, out_shape=tuple((jax.ShapeDtypeStruct(a.shap...  1.02 us

profile of v4, /device:TPU:1, one launch (start us, length us, event | category | flops | bytes accessed | tf_op | source)
XLA Modules:
  0.0 37.3 jit_solution(9537485445758271955)
XLA Ops:
  0.6 0.0 copy-start.1
  0.6 0.0 copy-start.2
  0.7 0.0 copy-start
  0.7 0.7 %copy-done.1 = f32[216]{0:T(256)S(1)} copy-done((f32[216]{0:T(256)S(1)}, f32[216]{0:T(256)}, u32[]{:S(2)}) %copy-start.1) | copy-done | bytes 888
  1.3 0.0 copy-done.2
  1.3 0.0 copy-done
  1.3 34.9 %shard_map.92 = (bf16[4,16,4096]{2,1,0:T(8,128)(2,1)S(1)}, bf16[4,16,4096]{2,1,0:T(8,128)(2,1)S(1)}, f32[1,216]{1,0:T(1,128)S(1)}, f32[1,216]{1,0:T(1,128)S(1)}, f32[1,216]{1,0:T(1,128)S(1)}) custom-call(bf16[4,16,4096]{2,1,0:T(8,128)(2,1)} %bitcast.13, bf16[4,16,4096]{2,1,0:T(8,128)(2,1)} %bitcast.14, f32[1,216]{1,0:T(1,128)S(1)} %bitcast.10, ...), custom_call_target="tpu_custom_call" | custom-call | tf_op jit(solution)/shard_map/pallas_call | solution.py:374
  36.3 1.0 %shard_map.93 = (bf16[4,16,4096]{2,1,0:T(8,128)(2,1)}, bf16[4,16,4096]{2,1,0:T(8,128)(2,1)}, f32[1,216]{1,0:T(1,128)}, f32[1,216]{1,0:T(1,128)}, f32[1,216]{1,0:T(1,128)}) custom-call(bf16[4,16,4096]{2,1,0:T(8,128)(2,1)S(1)} %get-tuple-element.15.refs_0_, bf16[4,16,4096]{2,1,0:T(8,128)(2,1)S(1)} %get-tuple-element.16.refs_1_, ...), custom_call_target="tpu_custom_call" | custom-call | tf_op jit(solution)/shard_map/pallas_call | solution.py:426
Async XLA Ops:
  0.6 0.7 %copy-start.1 = (f32[216]{0:T(256)S(1)}, f32[216]{0:T(256)}, u32[]{:S(2)}) copy-start(f32[216]{0:T(256)} %param.8) | copy-start | bytes 2596
  0.6 0.7 %copy-start.2 = (f32[216]{0:T(256)S(1)}, f32[216]{0:T(256)}, u32[]{:S(2)}) copy-start(f32[216]{0:T(256)} %param.9) | copy-start | bytes 2596
  0.7 0.7 %copy-start = (f32[216]{0:T(256)S(1)}, f32[216]{0:T(256)}, u32[]{:S(2)}) copy-start(f32[216]{0:T(256)} %param.7) | copy-start | bytes 2596

commit v5 on v4

--- a/solution.py
+++ b/solution.py
@@ -157,22 +157,21 @@
             flat[row + 128 : row + 192, :] = both[:, 0:128]
 
 
-def to_shares(flat, shares):
+def to_shares(flat, shares, zh):
     lane = iota((32, 128), 1)
-    for zh in range(2):
-        source = [flat[pl.ds(27 * zh + r, 32, stride=54), :] for r in range(27)]
-        for s in range(8):
-            halves = [jnp.zeros((32, 128), F32), jnp.zeros((32, 128), F32)]
-            for r in range(SHARE * s // 64, (SHARE * s + SHARE - 1) // 64 + 1):
-                at = 64 * r - SHARE * s
-                moved = pltpu.roll(source[r], at % 128, 1) if at % 128 else source[r]
-                low, high = max(at, 0), min(at + 64, SHARE)
-                for h in range(2):
-                    begin, end = max(low - 128 * h, 0), min(high - 128 * h, 128)
-                    if begin < end:
-                        halves[h] = jnp.where((lane >= begin) & (lane < end), moved, halves[h])
+    source = [flat[pl.ds(27 * zh + r, 32, stride=54), :] for r in range(27)]
+    for s in range(8):
+        halves = [jnp.zeros((32, 128), F32), jnp.zeros((32, 128), F32)]
+        for r in range(SHARE * s // 64, (SHARE * s + SHARE - 1) // 64 + 1):
+            at = 64 * r - SHARE * s
+            moved = pltpu.roll(source[r], at % 128, 1) if at % 128 else source[r]
+            low, high = max(at, 0), min(at + 64, SHARE)
             for h in range(2):
-                shares[s % 2, zh * 4 + s // 2, :, 128 * h : 128 * h + 128] = halves[h]
+                begin, end = max(low - 128 * h, 0), min(high - 128 * h, 128)
+                if begin < end:
+                    halves[h] = jnp.where((lane >= begin) & (lane < end), moved, halves[h])
+        for h in range(2):
+            shares[s % 2, zh * 4 + s // 2, :, 128 * h : 128 * h + 128] = halves[h]
 
 
 def from_shares(shares, flat):
@@ -290,13 +289,13 @@
         turn(act_pad, turned, p)
     pl.semaphore_wait(barrier, len(peers))
 
+    own = rows.at[me["z_row"], me["x"]]
+    gather_x = start([remote(row.at[0], own, gx, k, x_peer(me, d)) for k, d in enumerate(X)])
     greet(1)
     cot_halo = start([
         remote(cot_pad.at[4], cot_pad.at[0], hs, 0, slab_peer(me, 1)),
         remote(cot_pad.at[1], cot_pad.at[5], hs, 1, slab_peer(me, 7)),
     ])
-    own = rows.at[me["z_row"], me["x"]]
-    gather_x = start([remote(row.at[0], own, gx, k, x_peer(me, d)) for k, d in enumerate(X)])
     kernel_gradient(turned, b3, total, (2, 3, 1, 4))
     fold(total, flat, (1,))
     wait_recv(gather_x)
@@ -315,10 +314,20 @@
     edges(cot_pad, b3)
     kernel_gradient(turned, b3, total, (0, 5))
     fold(total, flat, (0, 2))
-    to_shares(flat, shares)
-    sum_core = start([remote(shares.at[1 - me["core"]], got, rc, 0, core_peer(me))])
-    wait_recv(sum_core)
+    sum_core = []
+    for zh in range(2):
+        to_shares(flat, shares, zh)
+        half = pl.ds(4 * zh, 4)
+        sum_core += start([remote(shares.at[1 - me["core"], half], got.at[half], rc, zh, core_peer(me))])
+    greeted(0)
+    wait_recv(gather_z)
+    wide[me["core"], me["y"]] = jnp.concatenate([rows[k // 4, k % 4] for k in range(32)], axis=0).astype(BF16)
+    block = wide.at[me["core"], me["y"]]
+    gather_y = start([remote(block, block, gy, k, y_peer(me, d)) for k, d in enumerate(EIGHT)])
+    gather_core = start([remote(block, block, gc, 7, core_peer(me))])
     for k in range(8):
+        if k % 4 == 0:
+            wait_recv([sum_core[k // 4]])
         both = shares[me["core"], k] + got[k]
         mine[k] = both
         sent[k] = both.astype(BF16)
@@ -326,14 +335,13 @@
         remote(sent.at[(me["z"] + d) % 8], parts.at[k], rz, k, z_peer(me, d)) for k, d in enumerate(EIGHT)
     ])
 
-    greeted(0)
-    wait_recv(gather_z)
-    wide[me["core"], me["y"]] = jnp.concatenate([rows[k // 4, k % 4] for k in range(32)], axis=0).astype(BF16)
-    block = wide.at[me["core"], me["y"]]
-    gather_y = start([remote(block, block, gy, k, y_peer(me, d)) for k, d in enumerate(EIGHT)])
     wait_recv(act_halo)
     edges(act_pad, a3)
 
+    for k in reversed(range(7)):
+        wait_recv([gather_y[k]])
+        landed = wide.at[me["core"], (me["y"] + 8 - EIGHT[k]) % 8]
+        gather_core += start([remote(landed, landed, gc, k, core_peer(me))])
     wait_recv(sum_z)
     summed = mine[me["z"]]
     for k in range(7):
@@ -343,9 +351,6 @@
     sum_xy = [remote(terms.at[xy_row(me, o)], term_parts.at[k], rx, 0, xy_peer(me, o)) for k, o in enumerate(XY)]
     start(sum_xy)
     all_xy = remote(term_parts, term_parts, rx, 0, xy_peer(me, XY[0]))
-    wait_recv(gather_y)
-    half = wide.at[me["core"]]
-    gather_core = start([remote(half, half, gc, 0, core_peer(me))])
     wait_recv(gather_core)
     from_shares(wide, flat)
     bands(flat, forward, backward)
@@ -403,8 +408,8 @@
             pltpu.SemaphoreType.DMA((2, 3)),
             pltpu.SemaphoreType.DMA((2, 7)),
             pltpu.SemaphoreType.DMA((2, 7)),
-            pltpu.SemaphoreType.DMA((2, 1)),
-            pltpu.SemaphoreType.DMA((2, 1)),
+            pltpu.SemaphoreType.DMA((2, 8)),
+            pltpu.SemaphoreType.DMA((2, 2)),
             pltpu.SemaphoreType.DMA((2, 7)),
             pltpu.SemaphoreType.DMA((2, 1)),
         ],

time: 37.5 us -> 36.6 us (0.976)
  Pallas kernels: 36 us -> 35.1 us
    pallas_call x1, Pallas kernels: 34.9 us -> 34 us  [step(): pl.pallas_call(step_kernel, out_shape=(planes, planes) + (share,) * 3, in...]
where the time goes in v5:
time: 36.6 us; the launch traced here: 36.4 us
  Pallas kernels  35.1 us (96%)
  local copies, waits for them, and re-layouts  0.69 us (2%)
  between operations  0.67 us (2%)
    pallas_call x1, Pallas kernels, step(): pl.pallas_call(step_kernel, out_shape=(planes, planes) + (share,) * 3, in...  34 us
    pallas_call x1, Pallas kernels, place_outputs(): pl.pallas_call(place_kernel, out_shape=tuple((jax.ShapeDtypeStruct(a.shap...  1.02 us

profile of v5, /device:TPU:1, one launch (start us, length us, event | category | flops | bytes accessed | tf_op | source)
XLA Modules:
  0.0 36.4 jit_solution(2753567043020966150)
XLA Ops:
  0.6 0.0 copy-start.1
  0.6 0.0 copy-start.2
  0.7 0.0 copy-start
  0.7 0.7 %copy-done.1 = f32[216]{0:T(256)S(1)} copy-done((f32[216]{0:T(256)S(1)}, f32[216]{0:T(256)}, u32[]{:S(2)}) %copy-start.1) | copy-done | bytes 888
  1.3 0.0 copy-done.2
  1.3 0.0 copy-done
  1.3 34.0 %shard_map.92 = (bf16[4,16,4096]{2,1,0:T(8,128)(2,1)S(1)}, bf16[4,16,4096]{2,1,0:T(8,128)(2,1)S(1)}, f32[1,216]{1,0:T(1,128)S(1)}, f32[1,216]{1,0:T(1,128)S(1)}, f32[1,216]{1,0:T(1,128)S(1)}) custom-call(bf16[4,16,4096]{2,1,0:T(8,128)(2,1)} %bitcast.13, bf16[4,16,4096]{2,1,0:T(8,128)(2,1)} %bitcast.14, f32[1,216]{1,0:T(1,128)S(1)} %bitcast.10, ...), custom_call_target="tpu_custom_call" | custom-call | tf_op jit(solution)/shard_map/pallas_call | solution.py:379
  35.4 1.0 %shard_map.93 = (bf16[4,16,4096]{2,1,0:T(8,128)(2,1)}, bf16[4,16,4096]{2,1,0:T(8,128)(2,1)}, f32[1,216]{1,0:T(1,128)}, f32[1,216]{1,0:T(1,128)}, f32[1,216]{1,0:T(1,128)}) custom-call(bf16[4,16,4096]{2,1,0:T(8,128)(2,1)S(1)} %get-tuple-element.15.refs_0_, bf16[4,16,4096]{2,1,0:T(8,128)(2,1)S(1)} %get-tuple-element.16.refs_1_, ...), custom_call_target="tpu_custom_call" | custom-call | tf_op jit(solution)/shard_map/pallas_call | solution.py:431
Async XLA Ops:
  0.6 0.7 %copy-start.1 = (f32[216]{0:T(256)S(1)}, f32[216]{0:T(256)}, u32[]{:S(2)}) copy-start(f32[216]{0:T(256)} %param.8) | copy-start | bytes 2596
  0.6 0.7 %copy-start.2 = (f32[216]{0:T(256)S(1)}, f32[216]{0:T(256)}, u32[]{:S(2)}) copy-start(f32[216]{0:T(256)} %param.9) | copy-start | bytes 2596
  0.7 0.7 %copy-start = (f32[216]{0:T(256)S(1)}, f32[216]{0:T(256)}, u32[]{:S(2)}) copy-start(f32[216]{0:T(256)} %param.7) | copy-start | bytes 2596

commit v6 on v5

--- a/solution.py
+++ b/solution.py
@@ -421,7 +421,9 @@
 
 def place_kernel(*refs):
     sems = refs[-1]
-    copies = start([pltpu.make_async_copy(refs[k], refs[k + 5], sems.at[k]) for k in range(5)])
+    pairs = [(refs[k].at[z], refs[k + 5].at[z]) for z in range(4) for k in range(2)]
+    pairs += [(refs[k], refs[k + 5]) for k in range(2, 5)]
+    copies = start([pltpu.make_async_copy(a, b, sems.at[n]) for n, (a, b) in enumerate(pairs)])
     for copy in copies:
         copy.wait()
 
@@ -433,7 +435,7 @@
         out_shape=tuple(jax.ShapeDtypeStruct(a.shape, a.dtype) for a in arrays),
         in_specs=[hbm] * 5,
         out_specs=(hbm,) * 5,
-        scratch_shapes=[pltpu.SemaphoreType.DMA((5,))],
+        scratch_shapes=[pltpu.SemaphoreType.DMA((11,))],
         compiler_params=pltpu.CompilerParams(vmem_limit_bytes=8 * 2**20),
     )(*arrays)
 

time: 36.6 us -> 36.6 us (level)
  no operation moved by 1% of the time
where the time goes in v6:
time: 36.6 us; the launch traced here: 36.4 us
  Pallas kernels  35.1 us (96%)
  local copies, waits for them, and re-layouts  0.69 us (2%)
  between operations  0.67 us (2%)
    pallas_call x1, Pallas kernels, step(): pl.pallas_call(step_kernel, out_shape=(planes, planes) + (share,) * 3, in...  34 us
    pallas_call x1, Pallas kernels, place_outputs(): pl.pallas_call(place_kernel, out_shape=tuple((jax.ShapeDtypeStruct(a.shap...  1.06 us

profile of v6, /device:TPU:1, one launch (start us, length us, event | category | flops | bytes accessed | tf_op | source)
XLA Modules:
  0.0 36.4 jit_solution(4167891874471719473)
XLA Ops:
  0.6 0.0 copy-start.1
  0.6 0.0 copy-start.2
  0.7 0.0 copy-start
  0.7 0.7 %copy-done.1 = f32[216]{0:T(256)S(1)} copy-done((f32[216]{0:T(256)S(1)}, f32[216]{0:T(256)}, u32[]{:S(2)}) %copy-start.1) | copy-done | bytes 888
  1.3 0.0 copy-done.2
  1.3 0.0 copy-done
  1.3 34.0 %shard_map.92 = (bf16[4,16,4096]{2,1,0:T(8,128)(2,1)S(1)}, bf16[4,16,4096]{2,1,0:T(8,128)(2,1)S(1)}, f32[1,216]{1,0:T(1,128)S(1)}, f32[1,216]{1,0:T(1,128)S(1)}, f32[1,216]{1,0:T(1,128)S(1)}) custom-call(bf16[4,16,4096]{2,1,0:T(8,128)(2,1)} %bitcast.13, bf16[4,16,4096]{2,1,0:T(8,128)(2,1)} %bitcast.14, f32[1,216]{1,0:T(1,128)S(1)} %bitcast.10, ...), custom_call_target="tpu_custom_call" | custom-call | tf_op jit(solution)/shard_map/pallas_call | solution.py:379
  35.4 1.1 %shard_map.93 = (bf16[4,16,4096]{2,1,0:T(8,128)(2,1)}, bf16[4,16,4096]{2,1,0:T(8,128)(2,1)}, f32[1,216]{1,0:T(1,128)}, f32[1,216]{1,0:T(1,128)}, f32[1,216]{1,0:T(1,128)}) custom-call(bf16[4,16,4096]{2,1,0:T(8,128)(2,1)S(1)} %get-tuple-element.15.refs_0_, bf16[4,16,4096]{2,1,0:T(8,128)(2,1)S(1)} %get-tuple-element.16.refs_1_, ...), custom_call_target="tpu_custom_call" | custom-call | tf_op jit(solution)/shard_map/pallas_call | solution.py:433
Async XLA Ops:
  0.6 0.7 %copy-start.1 = (f32[216]{0:T(256)S(1)}, f32[216]{0:T(256)}, u32[]{:S(2)}) copy-start(f32[216]{0:T(256)} %param.8) | copy-start | bytes 2596
  0.6 0.7 %copy-start.2 = (f32[216]{0:T(256)S(1)}, f32[216]{0:T(256)}, u32[]{:S(2)}) copy-start(f32[216]{0:T(256)} %param.9) | copy-start | bytes 2596
  0.7 0.7 %copy-start = (f32[216]{0:T(256)S(1)}, f32[216]{0:T(256)}, u32[]{:S(2)}) copy-start(f32[216]{0:T(256)} %param.7) | copy-start | bytes 2596
